TPU v7x, 128 devices: a whole 4x4x4 slice. The times are simulated.
128 devices in a mesh: fsdp: 128 (over x, y, z, core).
Axes of the slice: x: 4, y: 4, z: 4, core: 2. Of those that a mesh axis runs over, the one named last changes fastest.
Arguments:
- hidden_in: bfloat16 [65536, 768], P('fsdp'), may hold values from -6 to 6
- out_cotangent: bfloat16 [65536, 768], P('fsdp'), may hold values from -6 to 6
- lengths: int32 [256], replicated, may hold values from 1 to 511, as said below
- assignment: int32 [256], replicated, may hold values from 0 to 127
- qkv_weight: bfloat16 [768, 2304], P('fsdp'), may hold values from -0.21875 to 0.21875
- query_bias: bfloat16 [768], P('fsdp'), may hold values from -3 to 3
- value_bias: bfloat16 [768], P('fsdp'), may hold values from -3 to 3
- out_weight: bfloat16 [768, 768], P('fsdp'), may hold values from -2.5 to 2.5
- out_bias: bfloat16 [768], P('fsdp'), may hold values from -3 to 3
- first_gain: bfloat16 [768], P('fsdp'), may hold values from 0.5 to 1.5
- first_shift: bfloat16 [768], P('fsdp'), may hold values from -3 to 3
- in_weight: bfloat16 [768, 3072], P('fsdp'), may hold values from -0.21875 to 0.21875
- in_bias: bfloat16 [3072], P('fsdp'), may hold values from -3 to 3
- back_weight: bfloat16 [3072, 768], P('fsdp'), may hold values from -0.109375 to 0.109375
- back_bias: bfloat16 [768], P('fsdp'), may hold values from -3 to 3
- second_gain: bfloat16 [768], P('fsdp'), may hold values from 0.5 to 1.5
- second_shift: bfloat16 [768], P('fsdp'), may hold values from -3 to 3
Outputs:
- layer_out: bfloat16 [65536, 768], P('fsdp')
- input_grad: bfloat16 [65536, 768], P('fsdp')
- qkv_weight_grad: float32 [768, 2304], P('fsdp')
- query_bias_grad: float32 [768], P('fsdp')
- value_bias_grad: float32 [768], P('fsdp')
- out_weight_grad: float32 [768, 768], P('fsdp')
- out_bias_grad: float32 [768], P('fsdp')
- first_gain_grad: float32 [768], P('fsdp')
- first_shift_grad: float32 [768], P('fsdp')
- in_weight_grad: float32 [768, 3072], P('fsdp')
- in_bias_grad: float32 [3072], P('fsdp')
- back_weight_grad: float32 [3072, 768], P('fsdp')
- back_bias_grad: float32 [768], P('fsdp')
- second_gain_grad: float32 [768], P('fsdp')
- second_shift_grad: float32 [768], P('fsdp')
Inputs may be any that keep to these rules, and one draw needn't show every extreme that they name: Each device holds exactly 2 sequences; the lengths on one device sum to at most 512, and to exactly 512 on some device.
All inputs are finite; a program needn't handle non-finite values.
Results may differ from a plain program's by a relative error of at most 0.018.
Values may be sent and summed in bfloat16 or wider, within the bound.
No kernel may reach another device: no remote copies, remote signals or barrier semaphores. Data moves between devices by JAX's collectives and lax.ppermute only.
A program may use at most 192 MiB of HBM per device.

v0:
```python
import functools

import jax
import jax.numpy as jnp
from jax import lax
from jax.experimental import pallas as pl
from jax.experimental.pallas import tpu as pltpu
from jax.sharding import Mesh, PartitionSpec as P

ROWS = 512
D = 768
FF = 3072
LANES = 128
EPSILON = 1e-05
SCALE = 0.125
MASK_FILL = -1000000000.0
bf16, f32 = jnp.bfloat16, jnp.float32
NAMES = ("bq", "bv", "bo", "g1", "s1", "bi", "bb", "g2", "s2")
CUTS = dict(zip(NAMES, (6, 6, 6, 6, 6, 24, 6, 6, 6)))
AT = dict(zip(NAMES, (0, 6, 12, 18, 24, 30, 54, 60, 66)))
ROW_OF = dict(bq=0, bv=1, bo=2, g1=3, s1=4, bb=5, g2=6, s2=7)
LAST = (((1,), (1,)), ((), ()))
FIRST = (((0,), (0,)), ((), ()))


def shape(dims, kind=f32):
    return jax.ShapeDtypeStruct(dims, kind)


def whole(dims):
    return pl.BlockSpec(dims, lambda *_: (0,) * len(dims), pipeline_mode=pl.Buffered(1))


def kept(dims):
    return pl.BlockSpec(dims, lambda *_: (0,) * len(dims))


def run(kernel, grid, ins, outs, shapes, scratch=(), scalars=0, flops=0, size=0, alias=None):
    return pl.pallas_call(
        kernel,
        grid_spec=pltpu.PrefetchScalarGridSpec(
            num_scalar_prefetch=scalars,
            grid=grid,
            in_specs=ins,
            out_specs=outs,
            scratch_shapes=scratch,
        ),
        out_shape=shapes,
        input_output_aliases=alias or {},
        compiler_params=pltpu.CompilerParams(vmem_limit_bytes=63 * 1024 * 1024),
        cost_estimate=pl.CostEstimate(flops=flops, bytes_accessed=size, transcendentals=0),
    )


def mul(a, b, dims=(((1,), (0,)), ((), ()))):
    return lax.dot_general(a, b, dims, preferred_element_type=f32)


def shifted(n, step):
    return [(i, (i + step) % n) for i in range(n)]


def pack_kernel(place, qkv, out, inw, back, row, keep_o, send_o):
    halves = []
    for half in range(2):
        blocks = [(qkv, 6 * t + 3 * half + j) for t in range(3) for j in range(3)]
        blocks += [(out, 3 * half + j) for j in range(3)]
        blocks += [(inw, 12 * half + j) for j in range(12)]
        blocks += [(back, 3 * half + j) for j in range(3)]
        parts = [ref[:, LANES * j : LANES * (j + 1)].astype(f32) for ref, j in blocks]
        parts += [row[...].astype(f32), jnp.zeros((7, LANES), f32)]
        halves.append(jnp.concatenate(parts, axis=0).astype(bf16))
    for core in range(2):

        @pl.when(place[3] == core)
        def _():
            keep_o[...], send_o[...] = halves[core], halves[1 - core]


def pack(place, qkv, out, inw, back, row):
    arrays = (qkv, out, inw, back, row)
    return run(
        pack_kernel,
        (1,),
        [kept(a.shape) for a in arrays],
        [kept((224, LANES))] * 2,
        [shape((224, LANES), bf16)] * 2,
        scalars=1,
    )(place, *arrays)


def tile_kernel(place, *refs):
    ins, (one_o, two_o, rest_o, near) = refs[:4], refs[4:]
    core = place[3]
    for ref, k in zip(ins, (0, 1, 3, 2)):
        z = (place[2] + 4 - k) % 4
        near[z, core] = ref[:224, :].astype(f32)
        near[z, 1 - core] = ref[224:, :].astype(f32)

    def block(first, height):
        parts = [near[z, c, first : first + height, :] for z in range(4) for c in range(2)]
        return jnp.concatenate(parts, axis=0)

    head = [block(6 * i, 6) for i in range(12)] + [block(216, 1), jnp.zeros((8, LANES), f32)]
    head = jnp.concatenate(head, axis=0).astype(bf16)
    one_o[...], two_o[...] = head[:304], head[304:]
    rest = [block(6 * i, 6) for i in range(12, 24)] + [block(144 + 24 * j, 24) for j in range(3)]
    rest_o[...] = jnp.concatenate(rest, axis=0).astype(bf16)


def tile(place, parts):
    return run(
        tile_kernel,
        (1,),
        [kept((448, LANES))] * 4,
        [kept((304, LANES)), kept((288, LANES)), kept((1152, LANES))],
        [shape((304, LANES), bf16), shape((288, LANES), bf16), shape((1152, LANES), bf16)],
        [pltpu.VMEM((4, 2, 224, LANES), f32)],
        scalars=1,
    )(place, *parts)


def line_kernel(place, *refs):
    ins, outs = refs[:8], refs[8:]
    for out, first, at in ((outs[0], 0, place[0]), (outs[1], 4, place[1])):
        for i, k in enumerate((0, 1, 3, 2)):
            out[(at + 4 - k) % 4] = ins[first + i][...]


def line(place, parts):
    outs = [(4, *parts[0].shape), (4, *parts[4].shape)]
    return run(
        line_kernel,
        (1,),
        [kept(p.shape) for p in parts],
        [kept(o) for o in outs],
        [shape(o, bf16) for o in outs],
        scalars=1,
    )(place, *parts)


def plane_kernel(place, *refs):
    ins, out = refs[:8], refs[8]
    rows = ins[0].shape[1]
    for i, k in enumerate((0, 1, 3, 2)):
        x, y = (place[0] + 4 - k) % 4, (place[1] + 4 - k) % 4
        for j in range(4):
            out[4 * j + y, :rows, :] = ins[i][j]
            out[4 * x + j, rows:, :] = ins[4 + i][j]


def plane(place, parts):
    rows = parts[0].shape[1] + parts[4].shape[1]
    return run(
        plane_kernel,
        (1,),
        [kept(p.shape) for p in parts],
        kept((16, rows, LANES)),
        shape((16, rows, LANES), bf16),
        scalars=1,
    )(place, *parts)


def spread_along(value, axis):
    return [value] + [lax.ppermute(value, axis, shifted(4, k)) for k in (1, 3, 2)]


def gather_all(place, qkv, out, inw, back, small):
    row = sum(jnp.pad(v, (AT[n], LANES - AT[n] - CUTS[n])) for n, v in zip(NAMES, small))[None]
    keep, send = pack(place, qkv, out, inw, back, row)
    pair = jnp.concatenate([keep, swap(send)], axis=0)
    one, two, rest = tile(place, spread_along(pair, "z"))
    rest = lax.all_gather(rest, ("x", "y", "c"), tiled=False).reshape(16, 2, 1152, LANES)
    one, two = line(place, spread_along(one, "x") + spread_along(two, "y"))
    own = plane(place, spread_along(one, "y") + spread_along(two, "x"))
    return own, swap(own), rest


def chosen(here, own, other):
    rows = own.shape[0] * 48
    blocks = own.shape[1] // 48

    def of(ref):
        parts = [ref[:, 48 * j : 48 * (j + 1), :].reshape(rows, LANES) for j in range(blocks)]
        return parts[0] if blocks == 1 else jnp.concatenate(parts, axis=1)

    return lax.cond(here, lambda: of(own), lambda: of(other))


def held_columns(ref, block):
    rows = pl.ds(pl.multiple_of(48 * block, 16), 48)
    return ref[:, rows, :].reshape(D, LANES)


def out_columns(core, own, other):
    left, right = chosen(core == 0, own, other), chosen(core == 1, own, other)
    return jnp.concatenate([left, right], axis=1)


def columns(ref, count, height=48, halves=(0,)):
    rows = ref.shape[0] * height
    parts = [
        ref[:, half, height * j : height * (j + 1), :].reshape(rows, LANES)
        for half in halves
        for j in range(count)
    ]
    return parts[0] if len(parts) == 1 else jnp.concatenate(parts, axis=1)


OUT = pl.BlockSpec((16, 144, LANES), lambda *_: (0, 3, 0), pipeline_mode=pl.Buffered(1))
IN = pl.BlockSpec((16, 1, 144, LANES), lambda b: (0, b // 4, b % 4, 0))
BACK = pl.BlockSpec((2, 2, 576, LANES), lambda b: (b, 0, 1, 0))
ANYWHERE = pl.BlockSpec(memory_space=pl.ANY)
PAIR = pl.BlockSpec((ROWS, LANES), lambda p, *_: (0, p))
WIDE = pl.BlockSpec((ROWS, 384), lambda b: (0, b))


def place_of(cut, shape_, dim):
    at = lax.broadcasted_iota(jnp.int32, shape_, dim)
    owner = (at * (10923 if cut == 6 else 2731)) >> 16
    return owner, at - owner * cut


def spread(rows, name):
    cut = CUTS[name]
    width = cut * 128
    _, place = place_of(cut, (LANES, width), 1)
    pick = lax.broadcasted_iota(jnp.int32, (LANES, width), 0) == place + AT[name]
    every = mul(rows, jnp.where(pick, 1.0, 0.0).astype(bf16))
    owner, _ = place_of(cut, (128, width), 1)
    here = lax.broadcasted_iota(jnp.int32, (128, width), 0) == owner
    return jnp.sum(jnp.where(here, every, 0.0), axis=0, keepdims=True)


def gathered_rows(vectors):
    total = jnp.zeros((128, LANES), f32)
    for name, vector in vectors:
        cut = CUTS[name]
        width = cut * 128
        owner, _ = place_of(cut, (128, width), 1)
        here = lax.broadcasted_iota(jnp.int32, (128, width), 0) == owner
        _, place = place_of(cut, (width, LANES), 0)
        pick = lax.broadcasted_iota(jnp.int32, (width, LANES), 1) == place + AT[name]
        own = jnp.where(here, vector, 0.0).astype(bf16)
        total = total + mul(own, jnp.where(pick, 1.0, 0.0).astype(bf16))
    total = total.reshape(16, 8, LANES)
    return jnp.concatenate([total, jnp.zeros((16, 8, LANES), f32)], axis=1).astype(bf16)


def normalise(total):
    centred = total - jnp.mean(total, axis=-1, keepdims=True)
    inverse = lax.rsqrt(jnp.mean(centred * centred, axis=-1, keepdims=True) + EPSILON)
    return centred * inverse, inverse


def norm_back(grad, normed, inverse, gain):
    scaled = grad * gain
    mean = jnp.mean(scaled, axis=-1, keepdims=True)
    slope = jnp.mean(scaled * normed, axis=-1, keepdims=True)
    return inverse * (scaled - mean - normed * slope)


def column_sum(value):
    return jnp.sum(value, axis=0, keepdims=True)


def head_mask(head):
    lane = lax.broadcasted_iota(jnp.int32, (ROWS, LANES), 1)
    return (lane < 64) if head == 0 else (lane >= 64)


def masked(value, head, factor=1.0):
    return jnp.where(head_mask(head), value.astype(f32) * factor, 0.0).astype(bf16)


def attend_kernel(
    place, x, sc, sr, own, other, q_o, k_o, v_o, lse_o, ctx_o, n1_o, low_o, turn_o, inv_o, vec_o,
    bin_o, bias, ctx_s, held, arrived_s,
):
    p = pl.program_id(0)

    @pl.when(p == 0)
    def _():
        core = place[3]
        copies = [
            pltpu.make_async_copy(own, held.at[core], arrived_s.at[0]),
            pltpu.make_async_copy(other, held.at[1 - core], arrived_s.at[1]),
        ]
        for copy in copies:
            copy.start()
        bias[...] = jnp.where(sc[...] == sr[...], 0.0, MASK_FILL)
        for copy in copies:
            copy.wait()
        rows = held[0, :, 576:592, :].astype(f32)[:, :8, :].reshape(128, LANES).astype(bf16)
        for name, row in ROW_OF.items():
            vec_o[row : row + 1, :] = spread(rows, name)
        bin_o[0:1, :] = spread(rows, "bi")

    weights = [held_columns(held.at[p // 3], 3 * t + p % 3) for t in range(3)]
    mixed = mul(x[...], jnp.concatenate(weights, axis=1))
    lanes = pl.ds(pl.multiple_of(p * LANES, LANES), LANES)
    q = (mixed[:, :LANES] + vec_o[0:1, lanes]).astype(bf16)
    k = mixed[:, LANES : 2 * LANES].astype(bf16)
    value = (mixed[:, 2 * LANES :] + vec_o[1:2, lanes]).astype(bf16)
    q_o[...], k_o[...], v_o[...] = q, k, value
    turned = value.astype(f32).T.astype(bf16)
    parts = []
    for head in range(2):
        scores = mul(k, masked(q, head, SCALE), LAST) + bias[...]
        top = jnp.max(scores, axis=0, keepdims=True)
        raised = jnp.exp(scores - top)
        total = jnp.sum(raised, axis=0, keepdims=True)
        lse_o[0, head : head + 1, :] = top + jnp.log(total)
        probs = (raised * (1.0 / total)).astype(bf16)
        parts.append(mul(turned[64 * head : 64 * (head + 1)], probs))
    context = jnp.concatenate(parts, axis=0)
    ctx_o[...] = context.astype(bf16)
    ctx_s[:, lanes] = context.T.astype(bf16)

    @pl.when(p == 5)
    def _():
        weights = [held_columns(held.at[h], 9 + j) for h in range(2) for j in range(3)]
        attn = mul(ctx_s[...], jnp.concatenate(weights, axis=1)) + vec_o[2:3, :]
        normed, inverse = normalise(x[...].astype(f32) + attn)
        n1_o[...], inv_o[...] = normed, inverse
        first = normed * vec_o[3:4, :] + vec_o[4:5, :]
        low_o[...], turn_o[...] = first.astype(bf16), first.T.astype(bf16)


def attend(place, x, seg_col, seg_row, own, other):
    wide, tall, pair = shape((ROWS, D), bf16), shape((D, ROWS), bf16), PAIR
    return run(
        attend_kernel,
        (6,),
        [whole((ROWS, D)), whole((ROWS, 1)), whole((1, ROWS)), ANYWHERE, ANYWHERE],
        [pair, pair, pair, pl.BlockSpec((1, 8, ROWS), lambda p, *_: (p, 0, 0))]
        + [pl.BlockSpec((LANES, ROWS), lambda p, *_: (p, 0)), kept((ROWS, D)), kept((ROWS, D))]
        + [kept((D, ROWS)), kept((ROWS, 1)), kept((8, D)), kept((8, FF))],
        [wide, wide, wide, shape((6, 8, ROWS)), tall, shape((ROWS, D)), wide, tall]
        + [shape((ROWS, 1)), shape((8, D)), shape((8, FF))],
        [pltpu.VMEM((ROWS, ROWS), f32), pltpu.VMEM((ROWS, D), bf16)]
        + [pltpu.VMEM((2, 16, 592, LANES), bf16), pltpu.SemaphoreType.DMA((2,))],
        scalars=1,
        flops=6_000_000_000,
        size=12_000_000,
    )(place, x, seg_col, seg_row, own, other)


def forward_kernel(
    low, n1, sc, cot, vec, bi, wi, wb, act_o, slope_o, out_o, dsec_o, dbr_o, sums_o, acc
):
    b = pl.program_id(0)
    pre = mul(low[...], columns(wi, 3)) + bi[0:1, :]
    share = 0.5 * lax.erf(pre * 0.7071067811865476) + 0.5
    act = pre * share
    act_o[...] = act.T.astype(bf16)
    act = act.astype(bf16)
    slope_o[...] = (share + pre * (jnp.exp(pre * pre * -0.5) * 0.3989422804014327)).astype(bf16)
    term = mul(act, columns(wb, 3, 192, (0, 1)))

    @pl.when(b == 0)
    def _():
        acc[...] = term

    @pl.when(b > 0)
    def _():
        acc[...] += term

    @pl.when(b == 7)
    def _():
        first = n1[...] * vec[3:4, :] + vec[4:5, :]
        normed, inverse = normalise(first + (acc[...] + vec[5:6, :]))
        valid = jnp.where(sc[...] > 0, 1.0, 0.0)
        out_o[...] = ((normed * vec[6:7, :] + vec[7:8, :]) * valid).astype(bf16)
        grad = cot[...].astype(f32) * valid
        sums_o[0:1, :] = column_sum(grad * normed)
        sums_o[1:2, :] = column_sum(grad)
        second = norm_back(grad, normed, inverse, vec[6:7, :])
        dsec_o[...] = second
        rounded = second.astype(bf16)
        dbr_o[...] = rounded
        sums_o[2:3, :] = column_sum(rounded.astype(f32))


def forward(low, n1, seg_col, cot, vec, bi, gathered):
    deep, wide = shape((ROWS, FF), bf16), shape((ROWS, D), bf16)
    flat = whole((ROWS, D))
    return run(
        forward_kernel,
        (8,),
        [flat, flat, whole((ROWS, 1)), flat, whole((8, D))]
        + [pl.BlockSpec((8, 384), lambda b: (0, b)), IN, BACK],
        [pl.BlockSpec((384, ROWS), lambda b: (b, 0)), WIDE]
        + [kept((ROWS, D)), kept((ROWS, D)), kept((ROWS, D)), kept((8, D))],
        [shape((FF, ROWS), bf16), deep, wide, shape((ROWS, D)), wide, shape((8, D))],
        [pltpu.VMEM((ROWS, D), f32)],
        flops=10_000_000_000,
        size=20_000_000,
    )(low, n1, seg_col, cot, vec, bi, gathered, gathered)


def backward_one_kernel(dbr, slope, dsec, wi, wb, dpre_o, bi_o, acc):
    b = pl.program_id(0)
    dact = mul(dbr[...], columns(wb, 3, 192, (0, 1)), LAST)
    dpre = (dact * slope[...].astype(f32)).astype(bf16)
    dpre_o[...] = dpre
    bi_o[0:1, :] = column_sum(dpre.astype(f32))
    term = mul(dpre, columns(wi, 3), LAST)

    @pl.when(b == 0)
    def _():
        acc[...] = dsec[...] + term

    @pl.when(b > 0)
    def _():
        acc[...] += term


def backward_two_kernel(
    place, dbr, slope, dsec, wi, wb, wo, wo_2, n1, inv, vec, dpre_in, bi_in, dpre_o, bi_o, dfirst_o,
    dattn_o, dctx_o, sums_o, acc,
):
    backward_one_kernel(dbr, slope, dsec, wi, wb, dpre_o, bi_o, acc)

    @pl.when(pl.program_id(0) == 3)
    def _():
        grad, normed = acc[...], n1[...]
        sums_o[0:1, :] = column_sum(grad * normed)
        sums_o[1:2, :] = column_sum(grad)
        first = norm_back(grad, normed, inv[...], vec[3:4, :])
        dfirst_o[...] = first
        rounded = first.astype(bf16)
        dattn_o[...] = rounded
        sums_o[2:3, :] = column_sum(rounded.astype(f32))
        dctx_o[...] = mul(rounded, out_columns(place[3], wo, wo_2), LAST).astype(bf16)


def backward_specs(half):
    ins = [
        whole((ROWS, D)),
        pl.BlockSpec((ROWS, 384), lambda b, *_: (0, 4 * half + b)),
        whole((ROWS, D)),
        pl.BlockSpec((16, 1, 144, LANES), lambda b, *_: (0, half, b, 0)),
        pl.BlockSpec((2, 2, 576, LANES), lambda b, *_: (4 * half + b, 0, 1, 0)),
    ]
    outs = [
        pl.BlockSpec((ROWS, 384), lambda b, *_: (0, 4 * half + b)),
        pl.BlockSpec((8, 384), lambda b, *_: (0, 4 * half + b)),
    ]
    return ins, outs, [shape((ROWS, FF), bf16), shape((8, FF))]


def backward_one(dbr, slope, dsec, gathered):
    ins, outs, shapes = backward_specs(0)
    return run(
        backward_one_kernel,
        (4,),
        ins,
        outs + [kept((ROWS, D))],
        shapes + [shape((ROWS, D))],
        flops=5_000_000_000,
        size=10_000_000,
    )(dbr, slope, dsec, gathered, gathered)


def backward_two(place, dbr, slope, acc, n1, inv, vec, dpre, bi, gathered, own, other):
    wide, flat = shape((ROWS, D), bf16), whole((ROWS, D))
    ins, outs, shapes = backward_specs(1)
    return run(
        backward_two_kernel,
        (4,),
        ins + [OUT, OUT, flat, whole((ROWS, 1)), whole((8, D)), ANYWHERE, ANYWHERE],
        outs + [kept((ROWS, D)), kept((ROWS, D)), kept((ROWS, D)), kept((8, D))],
        shapes + [shape((ROWS, D)), wide, wide, shape((8, D))],
        [pltpu.VMEM((ROWS, D), f32)],
        flops=6_000_000_000,
        size=10_000_000,
        alias={11: 0, 12: 1},
        scalars=1,
    )(place, dbr, slope, acc, gathered, gathered, own, other, n1, inv, vec, dpre, bi)


def attend_back_kernel(
    half, place, q, k, v, dctx, lse, sc, sr, dfirst, own, other, mixed_o, sums_o, dx_o, bias, acc,
    held, arrived_s,
):
    p = pl.program_id(0)

    @pl.when(p == 0)
    def _():
        bias[...] = jnp.where(sc[...] == sr[...], 0.0, MASK_FILL)
        acc[...] = dfirst[...]
        for here, source in ((half, own), (1 - half, other)):

            @pl.when(place[3] == here)
            def _():
                copy = pltpu.make_async_copy(source.at[:, :432, :], held, arrived_s.at[0])
                copy.start()
                copy.wait()

    key, value = k[...], v[...]
    turned = key.astype(f32).T.astype(bf16)
    dk = jnp.zeros((ROWS, LANES), f32)
    dv = jnp.zeros((ROWS, LANES), f32)
    parts = []
    for head in range(2):
        query = masked(q[...], head, SCALE)
        grad = masked(dctx[...], head)
        probs = jnp.exp(mul(key, query, LAST) + bias[...] - lse[0, head : head + 1, :])
        dprobs = mul(value, grad, LAST)
        dv = dv + mul(probs.astype(bf16), grad)
        dscores = (probs * (dprobs - column_sum(probs * dprobs))).astype(bf16)
        dk = dk + mul(dscores, query)
        parts.append(mul(turned[64 * head : 64 * (head + 1)], dscores))
    dq = (jnp.concatenate(parts, axis=0).T * SCALE).astype(bf16)
    dk, dv = dk.astype(bf16), dv.astype(bf16)
    mixed_o[0], mixed_o[1], mixed_o[2] = dq, dk, dv
    sums_o[0:1, :] = column_sum(dq.astype(f32))
    sums_o[1:2, :] = column_sum(dv.astype(f32))
    weight = jnp.concatenate([held_columns(held, 3 * t + p) for t in range(3)], axis=1)
    acc[...] += mul(jnp.concatenate([dq, dk, dv], axis=1), weight, LAST)

    @pl.when(p == 2)
    def _():
        dx_o[...] = acc[...].astype(dx_o.dtype)


def attend_back(half, place, q, k, v, dctx, lse, seg_col, seg_row, dfirst, own, other):
    pair = pl.BlockSpec((ROWS, LANES), lambda p, *_: (0, 3 * half + p))
    return run(
        functools.partial(attend_back_kernel, half),
        (3,),
        [pair, pair, pair, pair, pl.BlockSpec((1, 8, ROWS), lambda p, *_: (3 * half + p, 0, 0))]
        + [whole((ROWS, 1)), whole((1, ROWS)), whole((ROWS, D)), ANYWHERE, ANYWHERE],
        [pl.BlockSpec((3, ROWS, LANES), lambda p, *_: (0, 0, p))]
        + [pl.BlockSpec((8, LANES), lambda p, *_: (0, p)), kept((ROWS, D))],
        [shape((3, ROWS, 384), bf16), shape((8, 384)), shape((ROWS, D), (f32, bf16)[half])],
        [pltpu.VMEM((ROWS, ROWS), f32), pltpu.VMEM((ROWS, D), f32)]
        + [pltpu.VMEM((16, 432, LANES), bf16), pltpu.SemaphoreType.DMA((1,))],
        scalars=1,
        flops=6_000_000_000,
        size=8_000_000,
    )(place, q, k, v, dctx, lse, seg_col, seg_row, dfirst, own, other)


def put(total, at, grad):
    rows = grad.astype(bf16).reshape(16, 48, -1)
    for j in range(rows.shape[2] // LANES):
        total[:, pl.ds(at + 48 * j, 48), :] = rows[:, :, LANES * j : LANES * (j + 1)]


def back_grad_kernel(place, act, act_2, dbr, dbr_2, total):
    grad = (mul(act[...], dbr[...]) + mul(act_2[...], dbr_2[...])).astype(bf16)
    for at in range(2):
        for j in range(3):
            part = grad[192 * at : 192 * (at + 1), LANES * j : LANES * (j + 1)]
            total[at, 192 * j : 192 * (j + 1), :] = part

def back_grad(place, act, act_2, dbr, dbr_2):
    tall = pl.BlockSpec((384, ROWS), lambda b, p: (b, 0))
    half = pl.BlockSpec((ROWS, 384), lambda b, p: (0, p[3]))
    return run(
        back_grad_kernel,
        (8,),
        [tall, tall, half, half],
        pl.BlockSpec((2, 576, LANES), lambda b, p: (b, 0, 0)),
        shape((16, 576, LANES), bf16),
        scalars=1,
        flops=2_400_000_000,
        size=10_000_000,
    )(place, act, act_2, dbr, dbr_2)


def middle_grad_kernel(
    place, low, low_2, dpre, dpre_2, ctx, ctx_2, dattn, dattn_2, two, bi, one, total
):
    b = pl.program_id(0)

    @pl.when(b < 4)
    def _():
        grad = mul(low[...], dpre[...]) + mul(low_2[...], dpre_2[...])
        put(total, pl.multiple_of(144 * b, 16), grad)

    @pl.when(b == 4)
    def _():
        put(total, 576, mul(ctx[...], dattn[...]) + mul(ctx_2[...], dattn_2[...]))
        names = (("g2", two, 0), ("s2", two, 1), ("bb", two, 2), ("bi", bi, 0))
        names = names + (("g1", one, 0), ("s1", one, 1), ("bo", one, 2))
        total[:, 720:736, :] = gathered_rows([(n, ref[i : i + 1, :]) for n, ref, i in names])


def middle_grad(place, low, low_2, dpre, dpre_2, ctx, ctx_2, dattn, dattn_2, two, bi, one):
    tall = whole((D, ROWS))
    quarter = pl.BlockSpec((ROWS, 384), lambda b, p: (0, 4 * p[3] + jnp.minimum(b, 3)))
    half = pl.BlockSpec((ROWS, 384), lambda b, p: (0, p[3]))
    return run(
        middle_grad_kernel,
        (5,),
        [tall, tall, quarter, quarter, tall, tall, half, half]
        + [whole((8, D)), whole((8, FF)), whole((8, D))],
        kept((16, 736, LANES)),
        shape((16, 736, LANES), bf16),
        scalars=1,
        flops=3_200_000_000,
        size=12_000_000,
    )(place, low, low_2, dpre, dpre_2, ctx, ctx_2, dattn, dattn_2, two, bi, one)


def qkv_grad_kernel(place, x, x_2, left, left_2, right, right_2, sums_l, sums_r, total):
    for core, own, other in ((0, left, left_2), (1, right, right_2)):

        @pl.when(place[3] == core)
        def _():
            for t in range(3):
                put(total, 144 * t, mul(x[...], own[t]) + mul(x_2[...], other[t]))

    sums = [jnp.concatenate([sums_l[i : i + 1, :], sums_r[i : i + 1, :]], axis=1) for i in (0, 1)]
    total[:, 432:448, :] = gathered_rows([("bq", sums[0]), ("bv", sums[1])])


def qkv_grad(place, x, x_2, left, left_2, right, right_2, sums_l, sums_r):
    half = kept((3, ROWS, 384))
    return run(
        qkv_grad_kernel,
        (1,),
        [kept((D, ROWS)), kept((D, ROWS)), half, half, half, half, kept((8, 384)), kept((8, 384))],
        kept((16, 448, LANES)),
        shape((16, 448, LANES), bf16),
        scalars=1,
        flops=1_800_000_000,
        size=7_000_000,
    )(place, x, x_2, left, left_2, right, right_2, sums_l, sums_r)


def last_kernel(place, *refs):
    early, late, outs = refs[0], refs[1], refs[2:]
    back, middle = early[:576, :].astype(f32), early[576:, :].astype(f32)
    qkv = late[0].astype(f32)
    for i in range(1, 16):
        qkv = qkv + late[i].astype(f32)
    wide = [qkv[48 * j : 48 * (j + 1)] for j in range(9)]
    wide = wide + [middle[576 + 48 * j : 576 + 48 * (j + 1)] for j in range(3)]
    wide = wide + [middle[48 * j : 48 * (j + 1)] for j in range(12)]
    rows = middle[720:728] + qkv[432:440]
    none = jnp.zeros((4, LANES), f32)
    for z in range(4):
        parts = []
        for block in wide:
            parts = parts + [block[12 * z : 12 * (z + 1)], none]
        for j in range(3):
            parts.append(back[192 * j + 48 * z : 192 * j + 48 * (z + 1)])
        parts = parts + [rows[2 * z : 2 * (z + 1)], jnp.zeros((14, LANES), f32)]
        total = jnp.concatenate(parts, axis=0).astype(bf16)
        for k in range(4):

            @pl.when((place[2] + k) % 4 == z)
            def _():
                outs[k][...] = total


def last_sum(place, parts):
    return run(
        last_kernel,
        (1,),
        [kept(p.shape) for p in parts],
        [kept((544, LANES))] * 4,
        [shape((544, LANES), bf16)] * 4,
        scalars=1,
        size=4_000_000,
    )(place, *parts)


def around(parts, axis):
    return [parts[0]] + [lax.ppermute(parts[k], axis, shifted(4, k)) for k in (1, 3, 2)]


def scattered(value, axis):
    return lax.psum_scatter(value, axis, tiled=True)


def swap(value):
    return lax.ppermute(value, "c", shifted(2, 1))


def together(*values):
    flat, tree = jax.tree.flatten(values)
    return jax.tree.unflatten(tree, lax.optimization_barrier(tuple(flat)))


def finish(place, core, parts):
    parts = around(last_sum(place, parts), "z")
    total = sum(p.astype(f32) for p in parts)
    wide = total[:384].reshape(24, 16, LANES)[:, :12].reshape(24, 2, 6, LANES)
    tall = total[384:528].reshape(3, 2, 24, LANES)

    def for_core(which):
        a = lax.dynamic_index_in_dim(wide, which, 1, keepdims=False).reshape(144, LANES)
        b = lax.dynamic_index_in_dim(tall, which, 1, keepdims=False).reshape(72, LANES)
        row = lax.dynamic_index_in_dim(total[528:530], which, 0)
        return jnp.concatenate([a, b, row], axis=0)

    own = for_core(core)
    other = lax.ppermute(for_core(1 - core).astype(bf16), "c", shifted(2, 1)).astype(f32)
    rows = own[216] + other[216]
    left, right = jnp.where(core == 0, own, other), jnp.where(core == 0, other, own)

    def joined(first, count, height, groups=1):
        parts = [
            jnp.moveaxis(a[first : first + count * height].reshape(count, height, LANES), 0, 1)
            for a in (left, right)
        ]
        parts = [p.reshape(height, groups, -1) for p in parts]
        return jnp.concatenate(parts, axis=2).reshape(height, -1)

    weights = joined(0, 9, 6, 3), joined(54, 3, 6), joined(72, 12, 6), joined(144, 3, 24)
    return weights, {n: rows[AT[n] : AT[n] + CUTS[n]] for n in NAMES}


def segment_rows(lengths, assignment, device, rows):
    count = lengths.shape[0]
    order = jnp.arange(count, dtype=jnp.int32)
    same = assignment[:, None] == assignment[None, :]
    before = order[None, :] < order[:, None]
    offset = jnp.sum(jnp.where(same & before, lengths[None, :], 0), axis=1)
    places = jnp.arange(rows, dtype=jnp.int32)[:, None]
    inside = (
        (assignment[None, :] == device)
        & (places >= offset[None, :])
        & (places < (offset + lengths)[None, :])
    )
    return jnp.sum(jnp.where(inside, order[None, :] + 1, 0), axis=1)


def body(
    hidden_in,
    out_cotangent,
    lengths,
    assignment,
    qkv_weight,
    query_bias,
    value_bias,
    out_weight,
    out_bias,
    first_gain,
    first_shift,
    in_weight,
    in_bias,
    back_weight,
    back_bias,
    second_gain,
    second_shift,
):
    small = [
        query_bias,
        value_bias,
        out_bias,
        first_gain,
        first_shift,
        in_bias,
        back_bias,
        second_gain,
        second_shift,
    ]
    px, py, pz, core = (lax.axis_index(a) for a in ("x", "y", "z", "c"))
    place = jnp.stack([px, py, pz, core]).astype(jnp.int32)
    own, other, gathered = gather_all(
        place, qkv_weight, out_weight, in_weight, back_weight, small
    )
    segment = segment_rows(lengths, assignment, ((px * 4 + py) * 4 + pz) * 2 + core, ROWS)
    seg_col, seg_row = segment.reshape(ROWS, 1), segment.reshape(1, ROWS)
    turned = hidden_in.T
    q, k, v, lse, ctx, n1, low, low_t, inv, vec, bi = attend(
        place, hidden_in, seg_col, seg_row, own, other
    )
    turned_2, ctx_2, low_2 = swap(turned), swap(ctx), swap(low_t)
    act, slope, layer_out, dsec, dbr, two = forward(
        low, n1, seg_col, out_cotangent, vec, bi, gathered
    )
    act, dbr, turned_2, ctx_2, low_2 = together(act, dbr, turned_2, ctx_2, low_2)
    act_2, dbr_2 = swap(act), swap(dbr)
    dpre, dbi, acc = backward_one(dbr, slope, dsec, gathered)
    act_2, dbr_2, acc = together(act_2, dbr_2, acc)
    back = back_grad(place, act, act_2, dbr, dbr_2)
    back, acc = together(back, acc)
    back = scattered(back.reshape(-1, LANES), "x")
    dpre, dbi, dfirst, dattn, dctx, one = backward_two(
        place, dbr, slope, acc, n1, inv, vec, dpre, dbi, gathered, own, other
    )
    dpre_2, dattn_2 = swap(dpre), swap(dattn)
    middle = middle_grad(
        place, low_t, low_2, dpre, dpre_2, ctx, ctx_2, dattn, dattn_2, two, dbi, one
    )
    middle, dctx = together(middle, dctx)
    middle = scattered(middle.reshape(-1, LANES), "x")
    left, sums_l, acc = attend_back(
        0, place, q, k, v, dctx, lse, seg_col, seg_row, dfirst, own, other
    )
    left_2 = swap(left)
    right, sums_r, input_grad = attend_back(
        1, place, q, k, v, dctx, lse, seg_col, seg_row, acc, own, other
    )
    left_2, right = together(left_2, right)
    right_2 = swap(right)
    late = qkv_grad(place, turned, turned_2, left, left_2, right, right_2, sums_l, sums_r)
    back, middle, late = together(back, middle, late)
    early = [back.reshape(4, 576, LANES), middle.reshape(4, 736, LANES)]
    early, late = together(jnp.concatenate(early, axis=1).reshape(-1, LANES), late)
    parts = [scattered(early, "y"), lax.all_to_all(late, ("x", "y"), 0, 0, tiled=True)]
    weights, s = finish(place, core, parts)
    return (
        layer_out,
        input_grad,
        weights[0],
        s["bq"],
        s["bv"],
        weights[1],
        s["bo"],
        s["g1"],
        s["s1"],
        weights[2],
        s["bi"],
        weights[3],
        s["bb"],
        s["g2"],
        s["s2"],
    )


def solution(mesh):
    axes = ("x", "y", "z", "c")
    grid = Mesh(mesh.devices.reshape(4, 4, 4, 2), axes)
    two, one, every = P(axes, None), P(axes), P()
    in_specs = (two, two, every, every, two, one, one, two, one, one, one, two, one, two)
    in_specs = in_specs + (one, one, one)
    out_specs = (two, two, two, one, one, two, one, one, one, two, one, two, one, one, one)
    return jax.shard_map(body, mesh=grid, in_specs=in_specs, out_specs=out_specs, check_vma=False)
```

profile of v0, /device:TPU:1, one launch (start us, length us, event | category | flops | bytes accessed | tf_op | source)
XLA Modules:
  0.0 279.1 jit_solution(9564902709217504878)
XLA Ops:
  21.1 3.5 %collective-permute-done.3.refs_3_ = bf16[448,128]{1,0:T(8,128)(2,1)S(1)} collective-permute-done((bf16[448,128]{1,0:T(8,128)(2,1)S(1)}, bf16[448,128]{1,0:T(8,128)(2,1)S(1)}, u32[]{:S(2)}, u32[]{:S(2)}) %collective-permute-start.3) | collective-permute-done | bytes 114720 | tf_op jit(solution)/shard_map/ppermute | solution.py:165
  25.3 2.6 shard_map.281
  37.0 3.0 %collective-permute-done.9.refs_7_ = bf16[288,128]{1,0:T(8,128)(2,1)S(1)} collective-permute-done((bf16[288,128]{1,0:T(8,128)(2,1)}, bf16[288,128]{1,0:T(8,128)(2,1)S(1)}, u32[]{:S(2)}, u32[]{:S(2)}) %collective-permute-start.9) | collective-permute-done | bytes 73760 | tf_op jit(solution)/shard_map/ppermute | solution.py:165
  41.3 2.7 shard_map.282
  50.0 4.7 %collective-permute-done.13.refs_5_ = bf16[4,288,128]{2,1,0:T(8,128)(2,1)S(1)} collective-permute-done((bf16[4,288,128]{2,1,0:T(8,128)(2,1)}, bf16[4,288,128]{2,1,0:T(8,128)(2,1)S(1)}, u32[]{:S(2)}, u32[]{:S(2)}) %collective-permute-start.13) | collective-permute-done | bytes 294944 | tf_op jit(solution)/shard_map/ppermute | solution.py:165
  55.0 7.4 %collective-permute-done.15.refs_7_ = bf16[4,288,128]{2,1,0:T(8,128)(2,1)S(1)} collective-permute-done((bf16[4,288,128]{2,1,0:T(8,128)(2,1)}, bf16[4,288,128]{2,1,0:T(8,128)(2,1)S(1)}, u32[]{:S(2)}, u32[]{:S(2)}) %collective-permute-start.15) | collective-permute-done | bytes 294944 | tf_op jit(solution)/shard_map/ppermute | solution.py:165
  64.6 3.9 %shard_map.283.own.wo = bf16[16,592,128]{2,1,0:T(8,128)(2,1)} custom-call(s32[4]{0:T(128)} %pad_add_fusion.place, bf16[4,304,128]{2,1,0:T(8,128)(2,1)} %get-tuple-element.81.refs_0_, bf16[4,304,128]{2,1,0:T(8,128)(2,1)} %copy-done.4, bf16[4,304,128]{2,1,0:T(8,128)(2,1)} %copy-done.5, bf16[4,304,128]{2,1,0:T(8,128)(2,1)} %copy-done.6, ...), custom_call_target="tpu_custom_call" | custom-call | tf_op jit(solution)/shard_map/pallas_call | solution.py:154
  68.5 6.6 %collective-permute-start.16 = (bf16[16,592,128]{2,1,0:T(8,128)(2,1)}, bf16[16,592,128]{2,1,0:T(8,128)(2,1)}, u32[]{:S(2)}, u32[]{:S(2)}) collective-permute-start(bf16[16,592,128]{2,1,0:T(8,128)(2,1)} %shard_map.283.own.wo), channel_id=1, source_target_pairs={{0,1},{1,0},{2,3},{3,2},{4,5},{5,4},{6,7},{7,6},{8,9},{9,8},{10,11... | collective-permute-start | bytes 7274504 | tf_op jit(solution)/shard_map/ppermute | solution.py:682
  79.9 20.6 %shard_map.284 = (bf16[512,768]{1,0:T(8,128)(2,1)}, bf16[512,768]{1,0:T(8,128)(2,1)}, bf16[512,768]{1,0:T(8,128)(2,1)}, f32[6,8,512]{2,1,0:T(8,128)}, bf16[768,5...) custom-call(s32[4]{0:T(128)} %pad_add_fusion.place, ...), custom_call_target="tpu_custom_call" | custom-call | flops 6000000000 | bytes 12000000 | tf_op jit(solution)/shard_map/pallas_call | solution.py:332
  101.2 17.4 %shard_map.285 = (bf16[3072,512]{1,0:T(8,128)(2,1)}, bf16[512,3072]{1,0:T(8,128)(2,1)}, bf16[512,768]{1,0:T(8,128)(2,1)}, f32[512,768]{1,0:T(8,128)}, bf16[512,768]{1,0:T(8,128)(2,1)}, /*index=5*/f32[8,768]{1,0:T(8,128)}) custom-call(bf16[512,768]{1,0:T(8,128)(2,1)} %get-tuple-element.83.low, f32[512,768]{1,0:T(8,128)} %get-tuple-element.84.n1, ...), custom_call_target="tpu_custom_call" | custom-call | flops 10000000000 | bytes 20000000 | tf_op jit(solution)/shard_map/pallas_call | solution.py:388
  119.2 8.6 %shard_map.286 = (bf16[512,3072]{1,0:T(8,128)(2,1)}, f32[8,3072]{1,0:T(8,128)}, f32[512,768]{1,0:T(8,128)}) custom-call(bf16[512,768]{1,0:T(8,128)(2,1)} %get-tuple-element.97.dbr, bf16[512,3072]{1,0:T(8,128)(2,1)} %get-tuple-element.98.slope, f32[512,768]{1,0:T(8,128)} %get-tuple-element.100.dsec, bf16[16,2,1152,128]{3,2,1,0:T(8,128)(2,1)} %bitcast.84, ...), custom_call_target="tpu_custom_call" | custom-call | flops 5000000000 | bytes 10000000 | tf_op jit(solution)/shard_map/pallas_call | solution.py:455
  128.6 9.6 %shard_map.287 = bf16[16,576,128]{2,1,0:T(8,128)(2,1)} custom-call(s32[4]{0:T(128)} %pad_add_fusion.place, bf16[3072,512]{1,0:T(8,128)(2,1)} %get-tuple-element.99.act, bf16[3072,512]{1,0:T(8,128)(2,1)} %collective-permute-done.20.act_2, bf16[512,768]{1,0:T(8,128)(2,1)} %get-tuple-element.97.dbr, bf16[512,768]{1,0:T(8,128)(2,1)} %copy-done.3), custom_call_target="tpu_custom_call" | custom-call | flops 2400000000 | bytes 10000000 | tf_op jit(solution)/shard_map/pallas_call | solution.py:562
  138.5 13.0 %shard_map.288 = (bf16[512,3072]{1,0:T(8,128)(2,1)}, f32[8,3072]{1,0:T(8,128)}, f32[512,768]{1,0:T(8,128)}, bf16[512,768]{1,0:T(8,128)(2,1)}, bf16[512,768]{1,0:T(8,128)(2,1)}, /*index=5*/f32[8,768]{1,0:T(8,128)}) custom-call(s32[4]{0:T(128)} %pad_add_fusion.place, ...), custom_call_target="tpu_custom_call", output_to_operand_aliasing={{0}: (11, {}), {1}: (12, {})} | custom-call | flops 6000000000 | bytes 10000000 | tf_op jit(solution)/shard_map/pallas_call | solution.py:469
  152.1 6.1 %collective-permute-done.23.dattn_2 = bf16[512,768]{1,0:T(8,128)(2,1)S(1)} collective-permute-done((bf16[512,768]{1,0:T(8,128)(2,1)}, bf16[512,768]{1,0:T(8,128)(2,1)S(1)}, u32[]{:S(2)}, u32[]{:S(2)}) %collective-permute-start.23) | collective-permute-done | bytes 786464 | tf_op jit(solution)/shard_map/ppermute | solution.py:682
  159.1 11.1 %shard_map.289 = bf16[16,736,128]{2,1,0:T(8,128)(2,1)} custom-call(s32[4]{0:T(128)} %pad_add_fusion.place, bf16[768,512]{1,0:T(8,128)(2,1)} %get-tuple-element.92.low, bf16[768,512]{1,0:T(8,128)(2,1)} %collective-permute-done.19.low_2, bf16[512,3072]{1,0:T(8,128)(2,1)} %get-tuple-element.109.dpre, bf16[512,3072]{1,0:T(8,128)(2,1)} %collective-permute-done.22.dpre_2, ...), custom_call_target="tpu_custom_call" | custom-call | flops 3200000000 | bytes 12000000 | tf_op jit(solution)/shard_map/pallas_call | solution.py:596
  170.2 13.1 %shard_map.290 = (bf16[3,512,384]{2,1,0:T(8,128)(2,1)}, f32[8,384]{1,0:T(8,128)}, f32[512,768]{1,0:T(8,128)}) custom-call(s32[4]{0:T(128)} %pad_add_fusion.place, bf16[512,768]{1,0:T(8,128)(2,1)} %get-tuple-element.89.q, bf16[512,768]{1,0:T(8,128)(2,1)} %get-tuple-element.90.k, bf16[512,768]{1,0:T(8,128)(2,1)} %get-tuple-element.91.v, ...), custom_call_target="tpu_custom_call" | custom-call | flops 6000000000 | bytes 8000000 | tf_op jit(solution)/shard_map/pallas_call | solution.py:530
  183.6 12.6 %shard_map.291 = (bf16[3,512,384]{2,1,0:T(8,128)(2,1)}, f32[8,384]{1,0:T(8,128)}, bf16[512,768]{1,0:T(8,128)(2,1)}) custom-call(s32[4]{0:T(128)} %pad_add_fusion.place, bf16[512,768]{1,0:T(8,128)(2,1)} %get-tuple-element.89.q, bf16[512,768]{1,0:T(8,128)(2,1)} %get-tuple-element.90.k, bf16[512,768]{1,0:T(8,128)(2,1)} %get-tuple-element.91.v, ...), custom_call_target="tpu_custom_call" | custom-call | flops 6000000000 | bytes 8000000 | tf_op jit(solution)/shard_map/pallas_call | solution.py:530
  196.8 2.8 %collective-permute-done.25.right_2 = bf16[3,512,384]{2,1,0:T(8,128)(2,1)} collective-permute-done((bf16[3,512,384]{2,1,0:T(8,128)(2,1)}, bf16[3,512,384]{2,1,0:T(8,128)(2,1)}, u32[]{:S(2)}, u32[]{:S(2)}) %collective-permute-start.25) | collective-permute-done | bytes 1179680 | tf_op jit(solution)/shard_map/ppermute | solution.py:682
  199.6 7.7 %shard_map.292 = bf16[16,448,128]{2,1,0:T(8,128)(2,1)} custom-call(s32[4]{0:T(128)} %pad_add_fusion.place, bf16[768,512]{1,0:T(8,128)(2,1)} %bitcast.92, bf16[768,512]{1,0:T(8,128)(2,1)} %collective-permute-done.17.x_2, bf16[3,512,384]{2,1,0:T(8,128)(2,1)} %get-tuple-element.124.left, bf16[3,512,384]{2,1,0:T(8,128)(2,1)} %collective-permute-done.24.left_2, ...), custom_call_target="tpu_custom_call" | custom-call | flops 1800000000 | bytes 7000000 | tf_op jit(solution)/shard_map/pallas_call | solution.py:623
  210.8 29.1 %all_to_all.5.refs_1_ = bf16[16,448,128]{2,1,0:T(8,128)(2,1)} all-to-all(bf16[16,448,128]{2,1,0:T(8,128)(2,1)S(1)} %copy-done), channel_id=1, replica_groups=mesh['x'=4,'y'=4,'z'=4,'c'=2] {'x','y'}, dimensions={0} | all-to-all | bytes 3670016 | tf_op jit(solution)/shard_map/all_to_all | solution.py:808
  239.9 10.4 %reduce-scatter.8.cloned.1.call-done.refs_0_ = bf16[1312,128]{1,0:T(8,128)(2,1)} async-done(((bf16[5248,128]{1,0:T(8,128)(2,1)}), bf16[1312,128]{1,0:T(8,128)(2,1)}) %reduce-scatter.8.cloned.1.call-update) | async-done | bytes 335888 | tf_op jit(solution)/shard_map/reduce_scatter | solution.py:678
  250.3 3.7 %shard_map.293 = (bf16[544,128]{1,0:T(8,128)(2,1)}, bf16[544,128]{1,0:T(8,128)(2,1)}, bf16[544,128]{1,0:T(8,128)(2,1)}, bf16[544,128]{1,0:T(8,128)(2,1)}) custom-call(s32[4]{0:T(128)} %pad_add_fusion.place, bf16[1312,128]{1,0:T(8,128)(2,1)} %reduce-scatter.8.cloned.1.call-done.refs_0_, bf16[16,448,128]{2,1,0:T(8,128)(2,1)} %all_to_all.5.refs_1_), custom_call_target="tpu_custom_call" | custom-call | bytes 4000000 | tf_op jit(solution)/shard_map/pallas_call | solution.py:662
  259.6 3.8 %collective-permute-done.28 = bf16[544,128]{1,0:T(8,128)(2,1)S(1)} collective-permute-done((bf16[544,128]{1,0:T(8,128)(2,1)}, bf16[544,128]{1,0:T(8,128)(2,1)S(1)}, u32[]{:S(2)}, u32[]{:S(2)}) %collective-permute-start.28) | collective-permute-done | bytes 139296 | tf_op jit(solution)/shard_map/ppermute | solution.py:674
  264.6 2.9 %collective-permute-start.29 = (bf16[217,128]{1,0:T(8,128)(2,1)S(1)}, bf16[217,128]{1,0:T(8,128)(2,1)S(1)}, u32[]{:S(2)}, u32[]{:S(2)}) collective-permute-start(bf16[217,128]{1,0:T(8,128)(2,1)S(1)} %pad_maximum_fusion.2), channel_id=1, source_target_pairs={{0,1},{1,0},{2,3},{3,2},{4,5},{5,4},{6,7},{7,6},{8,9},{9,8},{10,11... | collective-permute-start | bytes 166664 | tf_op jit(solution)/shard_map/ppermute | solution.py:703
  (165 shorter events, 57.9 us)
Async XLA Ops:
  7.2 94.0 %all-gather.3.cloned.1.call-start = ((), (), s32[]{:S(2)}) async-start(), calls=%async_computation.7 | async-start | bytes 9732096 | tf_op jit(solution)/shard_map/all_gather | solution.py:173
  13.9 7.1 %collective-permute-start.1 = (bf16[448,128]{1,0:T(8,128)(2,1)S(1)}, bf16[448,128]{1,0:T(8,128)(2,1)S(1)}, u32[]{:S(2)}, u32[]{:S(2)}) collective-permute-start(bf16[448,128]{1,0:T(8,128)(2,1)S(1)} %constant_dynamic-update-slice_fusion.refs_0_), channel_id=1, source_target_pairs={{0,2},{2,4},{4,6},{6,0},{1,3},{3,5},{5,7},{7,1},{8,10},{10,12},{12... | collective-permute-start | bytes 344072 | tf_op jit(solution)/shard_map/ppermute | solution.py:165
  17.9 6.7 %collective-permute-start.3 = (bf16[448,128]{1,0:T(8,128)(2,1)S(1)}, bf16[448,128]{1,0:T(8,128)(2,1)S(1)}, u32[]{:S(2)}, u32[]{:S(2)}) collective-permute-start(bf16[448,128]{1,0:T(8,128)(2,1)S(1)} %constant_dynamic-update-slice_fusion.refs_0_), channel_id=1, source_target_pairs={{0,4},{2,6},{4,0},{6,2},{1,5},{3,7},{5,1},{7,3},{8,12},{10,14},{12... | collective-permute-start | bytes 344072 | tf_op jit(solution)/shard_map/ppermute | solution.py:165
  27.9 179.4 %reduce-scatter.4.cloned.1.call-start = ((), (), s32[]{:S(2)}) async-start(), calls=%async_computation.4 | async-start | bytes 2949120 | tf_op jit(solution)/shard_map/reduce_scatter | solution.py:678
  27.9 7.1 %collective-permute-start.7 = (bf16[288,128]{1,0:T(8,128)(2,1)}, bf16[288,128]{1,0:T(8,128)(2,1)S(1)}, u32[]{:S(2)}, u32[]{:S(2)}) collective-permute-start(bf16[288,128]{1,0:T(8,128)(2,1)} %get-tuple-element.80.refs_4_), channel_id=1, source_target_pairs={{0,8},{8,16},{16,24},{24,0},{1,9},{9,17},{17,25},{25,1},{2,10},{10... | collective-permute-start | bytes 221192 | tf_op jit(solution)/shard_map/ppermute | solution.py:165
  29.3 10.7 %collective-permute-start.4 = (bf16[304,128]{1,0:T(8,128)(2,1)}, bf16[304,128]{1,0:T(8,128)(2,1)S(1)}, u32[]{:S(2)}, u32[]{:S(2)}) collective-permute-start(bf16[304,128]{1,0:T(8,128)(2,1)} %get-tuple-element.79.refs_0_), channel_id=1, source_target_pairs={{0,32},{32,64},{64,96},{96,0},{1,33},{33,65},{65,97},{97,1},{2,34}... | collective-permute-start | bytes 233480 | tf_op jit(solution)/shard_map/ppermute | solution.py:165
  30.5 9.5 %collective-permute-start.5 = (bf16[304,128]{1,0:T(8,128)(2,1)}, bf16[304,128]{1,0:T(8,128)(2,1)S(1)}, u32[]{:S(2)}, u32[]{:S(2)}) collective-permute-start(bf16[304,128]{1,0:T(8,128)(2,1)} %get-tuple-element.79.refs_0_), channel_id=1, source_target_pairs={{0,96},{32,0},{64,32},{96,64},{1,97},{33,1},{65,33},{97,65},{2,98}... | collective-permute-start | bytes 233480 | tf_op jit(solution)/shard_map/ppermute | solution.py:165
  32.0 8.0 %collective-permute-start.6 = (bf16[304,128]{1,0:T(8,128)(2,1)}, bf16[304,128]{1,0:T(8,128)(2,1)S(1)}, u32[]{:S(2)}, u32[]{:S(2)}) collective-permute-start(bf16[304,128]{1,0:T(8,128)(2,1)} %get-tuple-element.79.refs_0_), channel_id=1, source_target_pairs={{0,64},{32,96},{64,0},{96,32},{1,65},{33,97},{65,1},{97,33},{2,66}... | collective-permute-start | bytes 233480 | tf_op jit(solution)/shard_map/ppermute | solution.py:165
  43.9 10.7 %collective-permute-start.13 = (bf16[4,288,128]{2,1,0:T(8,128)(2,1)}, bf16[4,288,128]{2,1,0:T(8,128)(2,1)S(1)}, u32[]{:S(2)}, u32[]{:S(2)}) collective-permute-start(bf16[4,288,128]{2,1,0:T(8,128)(2,1)} %get-tuple-element.82.refs_4_), channel_id=1, source_target_pairs={{0,32},{32,64},{64,96},{96,0},{1,33},{33,65},{65,97},{97,1},{2,34}... | collective-permute-start | bytes 884744 | tf_op jit(solution)/shard_map/ppermute | solution.py:165
  44.3 18.1 %collective-permute-start.10 = (bf16[4,304,128]{2,1,0:T(8,128)(2,1)}, bf16[4,304,128]{2,1,0:T(8,128)(2,1)S(1)}, u32[]{:S(2)}, u32[]{:S(2)}) collective-permute-start(bf16[4,304,128]{2,1,0:T(8,128)(2,1)} %get-tuple-element.81.refs_0_), channel_id=1, source_target_pairs={{0,8},{8,16},{16,24},{24,0},{1,9},{9,17},{17,25},{25,1},{2,10},{10... | collective-permute-start | bytes 933896 | tf_op jit(solution)/shard_map/ppermute | solution.py:165
  44.5 17.9 %collective-permute-start.11 = (bf16[4,304,128]{2,1,0:T(8,128)(2,1)}, bf16[4,304,128]{2,1,0:T(8,128)(2,1)S(1)}, u32[]{:S(2)}, u32[]{:S(2)}) collective-permute-start(bf16[4,304,128]{2,1,0:T(8,128)(2,1)} %get-tuple-element.81.refs_0_), channel_id=1, source_target_pairs={{0,24},{8,0},{16,8},{24,16},{1,25},{9,1},{17,9},{25,17},{2,26},{10... | collective-permute-start | bytes 933896 | tf_op jit(solution)/shard_map/ppermute | solution.py:165
  46.9 16.2 %collective-permute-start.12 = (bf16[4,304,128]{2,1,0:T(8,128)(2,1)}, bf16[4,304,128]{2,1,0:T(8,128)(2,1)S(1)}, u32[]{:S(2)}, u32[]{:S(2)}) collective-permute-start(bf16[4,304,128]{2,1,0:T(8,128)(2,1)} %get-tuple-element.81.refs_0_), channel_id=1, source_target_pairs={{0,16},{8,24},{16,0},{24,8},{1,17},{9,25},{17,1},{25,9},{2,18},{10... | collective-permute-start | bytes 933896 | tf_op jit(solution)/shard_map/ppermute | solution.py:165
  47.6 7.4 %collective-permute-start.14 = (bf16[4,288,128]{2,1,0:T(8,128)(2,1)}, bf16[4,288,128]{2,1,0:T(8,128)(2,1)S(1)}, u32[]{:S(2)}, u32[]{:S(2)}) collective-permute-start(bf16[4,288,128]{2,1,0:T(8,128)(2,1)} %get-tuple-element.82.refs_4_), channel_id=1, source_target_pairs={{0,96},{32,0},{64,32},{96,64},{1,97},{33,1},{65,33},{97,65},{2,98}... | collective-permute-start | bytes 884744 | tf_op jit(solution)/shard_map/ppermute | solution.py:165
  54.7 7.7 %collective-permute-start.15 = (bf16[4,288,128]{2,1,0:T(8,128)(2,1)}, bf16[4,288,128]{2,1,0:T(8,128)(2,1)S(1)}, u32[]{:S(2)}, u32[]{:S(2)}) collective-permute-start(bf16[4,288,128]{2,1,0:T(8,128)(2,1)} %get-tuple-element.82.refs_4_), channel_id=1, source_target_pairs={{0,64},{32,96},{64,0},{96,32},{1,65},{33,97},{65,1},{97,33},{2,66}... | collective-permute-start | bytes 884744 | tf_op jit(solution)/shard_map/ppermute | solution.py:165
  68.5 11.4 %collective-permute-start.16 = (bf16[16,592,128]{2,1,0:T(8,128)(2,1)}, bf16[16,592,128]{2,1,0:T(8,128)(2,1)}, u32[]{:S(2)}, u32[]{:S(2)}) collective-permute-start(bf16[16,592,128]{2,1,0:T(8,128)(2,1)} %shard_map.283.own.wo), channel_id=1, source_target_pairs={{0,1},{1,0},{2,3},{3,2},{4,5},{5,4},{6,7},{7,6},{8,9},{9,8},{10,11... | collective-permute-start | bytes 7274504 | tf_op jit(solution)/shard_map/ppermute | solution.py:682
  76.5 42.0 %collective-permute-start.17 = (bf16[768,512]{1,0:T(8,128)(2,1)S(1)}, bf16[768,512]{1,0:T(8,128)(2,1)}, u32[]{:S(2)}, u32[]{:S(2)}) collective-permute-start(bf16[768,512]{1,0:T(8,128)(2,1)S(1)} %bitcast.91), channel_id=1, source_target_pairs={{0,1},{1,0},{2,3},{3,2},{4,5},{5,4},{6,7},{7,6},{8,9},{9,8},{10,11... | collective-permute-start | bytes 2359304 | tf_op jit(solution)/shard_map/ppermute | solution.py:682
  100.6 18.0 %collective-permute-start.18 = (bf16[768,512]{1,0:T(8,128)(2,1)}, bf16[768,512]{1,0:T(8,128)(2,1)}, u32[]{:S(2)}, u32[]{:S(2)}) collective-permute-start(bf16[768,512]{1,0:T(8,128)(2,1)} %get-tuple-element.95.ctx), channel_id=1, source_target_pairs={{0,1},{1,0},{2,3},{3,2},{4,5},{5,4},{6,7},{7,6},{8,9},{9,8},{10,11... | collective-permute-start | bytes 2359304 | tf_op jit(solution)/shard_map/ppermute | solution.py:682
  100.8 17.8 %collective-permute-start.19 = (bf16[768,512]{1,0:T(8,128)(2,1)}, bf16[768,512]{1,0:T(8,128)(2,1)}, u32[]{:S(2)}, u32[]{:S(2)}) collective-permute-start(bf16[768,512]{1,0:T(8,128)(2,1)} %get-tuple-element.92.low), channel_id=1, source_target_pairs={{0,1},{1,0},{2,3},{3,2},{4,5},{5,4},{6,7},{7,6},{8,9},{9,8},{10,11... | collective-permute-start | bytes 2359304 | tf_op jit(solution)/shard_map/ppermute | solution.py:682
  118.6 9.2 %collective-permute-start.20 = (bf16[3072,512]{1,0:T(8,128)(2,1)}, bf16[3072,512]{1,0:T(8,128)(2,1)}, u32[]{:S(2)}, u32[]{:S(2)}) collective-permute-start(bf16[3072,512]{1,0:T(8,128)(2,1)} %get-tuple-element.99.act), channel_id=1, source_target_pairs={{0,1},{1,0},{2,3},{3,2},{4,5},{5,4},{6,7},{7,6},{8,9},{9,8},{10,11... | collective-permute-start | bytes 9437192 | tf_op jit(solution)/shard_map/ppermute | solution.py:682
  118.8 8.9 %collective-permute-start.21 = (bf16[512,768]{1,0:T(8,128)(2,1)}, bf16[512,768]{1,0:T(8,128)(2,1)S(1)}, u32[]{:S(2)}, u32[]{:S(2)}) collective-permute-start(bf16[512,768]{1,0:T(8,128)(2,1)} %get-tuple-element.97.dbr), channel_id=1, source_target_pairs={{0,1},{1,0},{2,3},{3,2},{4,5},{5,4},{6,7},{7,6},{8,9},{9,8},{10,11... | collective-permute-start | bytes 2359304 | tf_op jit(solution)/shard_map/ppermute | solution.py:682
  138.2 70.0 %reduce-scatter.6.cloned.1.call-start = ((), (), s32[]{:S(2)}) async-start(), calls=%async_computation.5 | async-start | bytes 3768320 | tf_op jit(solution)/shard_map/reduce_scatter | solution.py:678
  151.5 7.2 %collective-permute-start.22 = (bf16[512,3072]{1,0:T(8,128)(2,1)}, bf16[512,3072]{1,0:T(8,128)(2,1)}, u32[]{:S(2)}, u32[]{:S(2)}) collective-permute-start(bf16[512,3072]{1,0:T(8,128)(2,1)} %get-tuple-element.109.dpre), channel_id=1, source_target_pairs={{0,1},{1,0},{2,3},{3,2},{4,5},{5,4},{6,7},{7,6},{8,9},{9,8},{10,11... | collective-permute-start | bytes 9437192 | tf_op jit(solution)/shard_map/ppermute | solution.py:682
  170.2 80.1 %reduce-scatter.8.cloned.1.call-start = ((), (), s32[]{:S(2)}) async-start(), calls=%async_computation.6 | async-start | bytes 1679360 | tf_op jit(solution)/shard_map/reduce_scatter | solution.py:678
  183.3 12.8 %collective-permute-start.24 = (bf16[3,512,384]{2,1,0:T(8,128)(2,1)}, bf16[3,512,384]{2,1,0:T(8,128)(2,1)}, u32[]{:S(2)}, u32[]{:S(2)}) collective-permute-start(bf16[3,512,384]{2,1,0:T(8,128)(2,1)} %get-tuple-element.124.left), channel_id=1, source_target_pairs={{0,1},{1,0},{2,3},{3,2},{4,5},{5,4},{6,7},{7,6},{8,9},{9,8},{10,11... | collective-permute-start | bytes 3538952 | tf_op jit(solution)/shard_map/ppermute | solution.py:682
  (33 other events, 189.9 us)
Sparse Core Ops, SparseCore 0:
  28.0 59.1 all-gather.2
  138.3 30.4 reduce-scatter.3
  171.3 36.8 reduce-scatter.5
  210.9 39.3 reduce-scatter.7
where the time goes:
time: 280 us; the launch traced here: 279 us
  Pallas kernels  129 us (46%)
  waiting for transfers between devices  49.5 us (18%)
  starting transfers between devices  38.9 us (14%)
  blocking collectives  29.1 us (10%)
  between operations  14.3 us (5%)
  local copies, waits for them, and re-layouts  10.6 us (4%)
  other arithmetic  7.95 us (3%)
    all_to_all x1, blocking collectives, body(): lax.all_to_all(late, ('x', 'y'), 0, 0, tiled=True)  29.1 us
    pallas_call x2, Pallas kernels, attend_back(): run(functools.partial(attend_back_kernel, half), (3,), [pair, pair, pair,...  25.6 us
    ppermute x15, waiting for transfers between devices, spread_along(): lax.ppermute(value, axis, shifted(4, k))  20.9 us
    pallas_call x1, Pallas kernels, attend(): run(attend_kernel, (6,), [whole((ROWS, D)), whole((ROWS, 1)), whole((1, R...  20.6 us
    ppermute x15, starting transfers between devices, spread_along(): lax.ppermute(value, axis, shifted(4, k))  20.2 us
    pallas_call x1, Pallas kernels, forward(): run(forward_kernel, (8,), [flat, flat, whole((ROWS, 1)), flat, whole((8,...  17.4 us
    pallas_call x1, Pallas kernels, backward_two(): run(backward_two_kernel, (4,), ins + [OUT, OUT, flat, whole((ROWS, 1)), w...  13 us
    ppermute x11, waiting for transfers between devices, swap(): return lax.ppermute(value, 'c', shifted(2, 1))  11.4 us
  transfers between devices with their start and end apart: 34, of which 16 were waited for; matrix products, arithmetic and copies ran while one was open for 1% of the time, Pallas kernels for 40%

commit v1 on v0

--- a/solution.py
+++ b/solution.py
@@ -8,6 +8,7 @@
 from jax.sharding import Mesh, PartitionSpec as P
 
 ROWS = 512
+STEP = 768
 D = 768
 FF = 3072
 LANES = 128
@@ -47,7 +48,7 @@
         ),
         out_shape=shapes,
         input_output_aliases=alias or {},
-        compiler_params=pltpu.CompilerParams(vmem_limit_bytes=63 * 1024 * 1024),
+        compiler_params=pltpu.CompilerParams(vmem_limit_bytes=64 * 1024 * 1024),
         cost_estimate=pl.CostEstimate(flops=flops, bytes_accessed=size, transcendentals=0),
     )
 
@@ -101,10 +102,11 @@
         parts = [near[z, c, first : first + height, :] for z in range(4) for c in range(2)]
         return jnp.concatenate(parts, axis=0)
 
-    head = [block(6 * i, 6) for i in range(12)] + [block(216, 1), jnp.zeros((8, LANES), f32)]
+    head = [block(6 * i, 6) for i in range(9)] + [block(216, 1), jnp.zeros((8, LANES), f32)]
     head = jnp.concatenate(head, axis=0).astype(bf16)
-    one_o[...], two_o[...] = head[:304], head[304:]
+    one_o[...], two_o[...] = head[:224], head[224:]
     rest = [block(6 * i, 6) for i in range(12, 24)] + [block(144 + 24 * j, 24) for j in range(3)]
+    rest = rest + [block(6 * i, 6) for i in range(9, 12)]
     rest_o[...] = jnp.concatenate(rest, axis=0).astype(bf16)
 
 
@@ -113,8 +115,8 @@
         tile_kernel,
         (1,),
         [kept((448, LANES))] * 4,
-        [kept((304, LANES)), kept((288, LANES)), kept((1152, LANES))],
-        [shape((304, LANES), bf16), shape((288, LANES), bf16), shape((1152, LANES), bf16)],
+        [kept((224, LANES)), kept((224, LANES)), kept((1296, LANES))],
+        [shape((224, LANES), bf16), shape((224, LANES), bf16), shape((1296, LANES), bf16)],
         [pltpu.VMEM((4, 2, 224, LANES), f32)],
         scalars=1,
     )(place, *parts)
@@ -165,36 +167,21 @@
     return [value] + [lax.ppermute(value, axis, shifted(4, k)) for k in (1, 3, 2)]
 
 
-def gather_all(place, qkv, out, inw, back, small):
+def gather_all(place, qkv, out, inw, back, small, ready):
     row = sum(jnp.pad(v, (AT[n], LANES - AT[n] - CUTS[n])) for n, v in zip(NAMES, small))[None]
     keep, send = pack(place, qkv, out, inw, back, row)
     pair = jnp.concatenate([keep, swap(send)], axis=0)
     one, two, rest = tile(place, spread_along(pair, "z"))
-    rest = lax.all_gather(rest, ("x", "y", "c"), tiled=False).reshape(16, 2, 1152, LANES)
+    rest = lax.all_gather(rest, ("x", "y", "c"), tiled=False).reshape(16, 2, 1296, LANES)
     one, two = line(place, spread_along(one, "x") + spread_along(two, "y"))
-    own = plane(place, spread_along(one, "y") + spread_along(two, "x"))
-    return own, swap(own), rest
-
-
-def chosen(here, own, other):
-    rows = own.shape[0] * 48
-    blocks = own.shape[1] // 48
-
-    def of(ref):
-        parts = [ref[:, 48 * j : 48 * (j + 1), :].reshape(rows, LANES) for j in range(blocks)]
-        return parts[0] if blocks == 1 else jnp.concatenate(parts, axis=1)
-
-    return lax.cond(here, lambda: of(own), lambda: of(other))
+    parts, ready = together(spread_along(one, "y") + spread_along(two, "x"), ready)
+    own = plane(place, parts)
+    return own, swap(own), rest, ready
 
 
 def held_columns(ref, block):
     rows = pl.ds(pl.multiple_of(48 * block, 16), 48)
     return ref[:, rows, :].reshape(D, LANES)
-
-
-def out_columns(core, own, other):
-    left, right = chosen(core == 0, own, other), chosen(core == 1, own, other)
-    return jnp.concatenate([left, right], axis=1)
 
 
 def columns(ref, count, height=48, halves=(0,)):
@@ -207,12 +194,17 @@
     return parts[0] if len(parts) == 1 else jnp.concatenate(parts, axis=1)
 
 
-OUT = pl.BlockSpec((16, 144, LANES), lambda *_: (0, 3, 0), pipeline_mode=pl.Buffered(1))
-IN = pl.BlockSpec((16, 1, 144, LANES), lambda b: (0, b // 4, b % 4, 0))
-BACK = pl.BlockSpec((2, 2, 576, LANES), lambda b: (b, 0, 1, 0))
+OUT = pl.BlockSpec(
+    (16, 2, 144, LANES), lambda *_: (0, 0, 8, 0), pipeline_mode=pl.Buffered(1)
+)
+HALF_STEPS = FF // STEP // 2
+IN = pl.BlockSpec(
+    (16, 1, STEP * 3 // 8, LANES), lambda b: (0, b // HALF_STEPS, b % HALF_STEPS, 0)
+)
+BACK = pl.BlockSpec((STEP // 192, 2, 576, LANES), lambda b: (b, 0, 1, 0))
 ANYWHERE = pl.BlockSpec(memory_space=pl.ANY)
 PAIR = pl.BlockSpec((ROWS, LANES), lambda p, *_: (0, p))
-WIDE = pl.BlockSpec((ROWS, 384), lambda b: (0, b))
+WIDE = pl.BlockSpec((ROWS, STEP), lambda b: (0, b))
 
 
 def place_of(cut, shape_, dim):
@@ -274,8 +266,8 @@
 
 
 def attend_kernel(
-    place, x, sc, sr, own, other, q_o, k_o, v_o, lse_o, ctx_o, n1_o, low_o, turn_o, inv_o, vec_o,
-    bin_o, bias, ctx_s, held, arrived_s,
+    place, x, sc, sr, own, other, q_o, k_o, v_o, lse_o, ctx_o, turn_o, vec_o, bin_o, bias, held,
+    arrived_s,
 ):
     p = pl.program_id(0)
 
@@ -291,7 +283,7 @@
         bias[...] = jnp.where(sc[...] == sr[...], 0.0, MASK_FILL)
         for copy in copies:
             copy.wait()
-        rows = held[0, :, 576:592, :].astype(f32)[:, :8, :].reshape(128, LANES).astype(bf16)
+        rows = held[0, :, 432:448, :].astype(f32)[:, :8, :].reshape(128, LANES).astype(bf16)
         for name, row in ROW_OF.items():
             vec_o[row : row + 1, :] = spread(rows, name)
         bin_o[0:1, :] = spread(rows, "bi")
@@ -314,17 +306,7 @@
         probs = (raised * (1.0 / total)).astype(bf16)
         parts.append(mul(turned[64 * head : 64 * (head + 1)], probs))
     context = jnp.concatenate(parts, axis=0)
-    ctx_o[...] = context.astype(bf16)
-    ctx_s[:, lanes] = context.T.astype(bf16)
-
-    @pl.when(p == 5)
-    def _():
-        weights = [held_columns(held.at[h], 9 + j) for h in range(2) for j in range(3)]
-        attn = mul(ctx_s[...], jnp.concatenate(weights, axis=1)) + vec_o[2:3, :]
-        normed, inverse = normalise(x[...].astype(f32) + attn)
-        n1_o[...], inv_o[...] = normed, inverse
-        first = normed * vec_o[3:4, :] + vec_o[4:5, :]
-        low_o[...], turn_o[...] = first.astype(bf16), first.T.astype(bf16)
+    turn_o[...], ctx_o[...] = context.astype(bf16), context.T.astype(bf16)
 
 
 def attend(place, x, seg_col, seg_row, own, other):
@@ -333,13 +315,11 @@
         attend_kernel,
         (6,),
         [whole((ROWS, D)), whole((ROWS, 1)), whole((1, ROWS)), ANYWHERE, ANYWHERE],
-        [pair, pair, pair, pl.BlockSpec((1, 8, ROWS), lambda p, *_: (p, 0, 0))]
-        + [pl.BlockSpec((LANES, ROWS), lambda p, *_: (p, 0)), kept((ROWS, D)), kept((ROWS, D))]
-        + [kept((D, ROWS)), kept((ROWS, 1)), kept((8, D)), kept((8, FF))],
-        [wide, wide, wide, shape((6, 8, ROWS)), tall, shape((ROWS, D)), wide, tall]
-        + [shape((ROWS, 1)), shape((8, D)), shape((8, FF))],
-        [pltpu.VMEM((ROWS, ROWS), f32), pltpu.VMEM((ROWS, D), bf16)]
-        + [pltpu.VMEM((2, 16, 592, LANES), bf16), pltpu.SemaphoreType.DMA((2,))],
+        [pair, pair, pair, pl.BlockSpec((1, 8, ROWS), lambda p, *_: (p, 0, 0)), pair]
+        + [pl.BlockSpec((LANES, ROWS), lambda p, *_: (p, 0)), kept((8, D)), kept((8, FF))],
+        [wide, wide, wide, shape((6, 8, ROWS)), wide, tall, shape((8, D)), shape((8, FF))],
+        [pltpu.VMEM((ROWS, ROWS), f32), pltpu.VMEM((2, 16, 448, LANES), bf16)]
+        + [pltpu.SemaphoreType.DMA((2,))],
         scalars=1,
         flops=6_000_000_000,
         size=12_000_000,
@@ -347,10 +327,20 @@
 
 
 def forward_kernel(
-    low, n1, sc, cot, vec, bi, wi, wb, act_o, slope_o, out_o, dsec_o, dbr_o, sums_o, acc
+    x, ctx, sc, cot, vec, bi, wi, wb, wo, act_o, slope_o, out_o, dsec_o, dbr_o, sums_o, n1_o, low_o,
+    turn_o, inv_o, acc,
 ):
     b = pl.program_id(0)
-    pre = mul(low[...], columns(wi, 3)) + bi[0:1, :]
+
+    @pl.when(b == 0)
+    def _():
+        attn = mul(ctx[...], columns(wo, 3, halves=(0, 1))) + vec[2:3, :]
+        normed, inverse = normalise(x[...].astype(f32) + attn)
+        n1_o[...], inv_o[...] = normed, inverse
+        first = normed * vec[3:4, :] + vec[4:5, :]
+        low_o[...], turn_o[...] = first.astype(bf16), first.T.astype(bf16)
+
+    pre = mul(low_o[...], columns(wi, STEP // LANES)) + bi[0:1, :]
     share = 0.5 * lax.erf(pre * 0.7071067811865476) + 0.5
     act = pre * share
     act_o[...] = act.T.astype(bf16)
@@ -366,9 +356,9 @@
     def _():
         acc[...] += term
 
-    @pl.when(b == 7)
-    def _():
-        first = n1[...] * vec[3:4, :] + vec[4:5, :]
+    @pl.when(b == FF // STEP - 1)
+    def _():
+        first = n1_o[...] * vec[3:4, :] + vec[4:5, :]
         normed, inverse = normalise(first + (acc[...] + vec[5:6, :]))
         valid = jnp.where(sc[...] > 0, 1.0, 0.0)
         out_o[...] = ((normed * vec[6:7, :] + vec[7:8, :]) * valid).astype(bf16)
@@ -382,21 +372,22 @@
         sums_o[2:3, :] = column_sum(rounded.astype(f32))
 
 
-def forward(low, n1, seg_col, cot, vec, bi, gathered):
+def forward(x, ctx, seg_col, cot, vec, bi, gathered):
     deep, wide = shape((ROWS, FF), bf16), shape((ROWS, D), bf16)
-    flat = whole((ROWS, D))
+    flat, out, sums = whole((ROWS, D)), kept((ROWS, D)), kept((8, D))
     return run(
         forward_kernel,
-        (8,),
+        (FF // STEP,),
         [flat, flat, whole((ROWS, 1)), flat, whole((8, D))]
-        + [pl.BlockSpec((8, 384), lambda b: (0, b)), IN, BACK],
-        [pl.BlockSpec((384, ROWS), lambda b: (b, 0)), WIDE]
-        + [kept((ROWS, D)), kept((ROWS, D)), kept((ROWS, D)), kept((8, D))],
-        [shape((FF, ROWS), bf16), deep, wide, shape((ROWS, D)), wide, shape((8, D))],
+        + [pl.BlockSpec((8, STEP), lambda b: (0, b)), IN, BACK, OUT],
+        [pl.BlockSpec((STEP, ROWS), lambda b: (b, 0)), WIDE, out, out, out, sums]
+        + [out, out, kept((D, ROWS)), kept((ROWS, 1))],
+        [shape((FF, ROWS), bf16), deep, wide, shape((ROWS, D)), wide, shape((8, D))]
+        + [shape((ROWS, D)), wide, shape((D, ROWS), bf16), shape((ROWS, 1))],
         [pltpu.VMEM((ROWS, D), f32)],
         flops=10_000_000_000,
         size=20_000_000,
-    )(low, n1, seg_col, cot, vec, bi, gathered, gathered)
+    )(x, ctx, seg_col, cot, vec, bi, gathered, gathered, gathered)
 
 
 def backward_one_kernel(dbr, slope, dsec, wi, wb, dpre_o, bi_o, acc):
@@ -405,7 +396,7 @@
     dpre = (dact * slope[...].astype(f32)).astype(bf16)
     dpre_o[...] = dpre
     bi_o[0:1, :] = column_sum(dpre.astype(f32))
-    term = mul(dpre, columns(wi, 3), LAST)
+    term = mul(dpre, columns(wi, STEP // LANES), LAST)
 
     @pl.when(b == 0)
     def _():
@@ -417,12 +408,12 @@
 
 
 def backward_two_kernel(
-    place, dbr, slope, dsec, wi, wb, wo, wo_2, n1, inv, vec, dpre_in, bi_in, dpre_o, bi_o, dfirst_o,
-    dattn_o, dctx_o, sums_o, acc,
+    dbr, slope, dsec, wi, wb, wo, n1, inv, vec, dpre_in, bi_in, dpre_o, bi_o, dfirst_o, dattn_o,
+    dctx_o, sums_o, acc,
 ):
     backward_one_kernel(dbr, slope, dsec, wi, wb, dpre_o, bi_o, acc)
 
-    @pl.when(pl.program_id(0) == 3)
+    @pl.when(pl.program_id(0) == HALF_STEPS - 1)
     def _():
         grad, normed = acc[...], n1[...]
         sums_o[0:1, :] = column_sum(grad * normed)
@@ -432,20 +423,21 @@
         rounded = first.astype(bf16)
         dattn_o[...] = rounded
         sums_o[2:3, :] = column_sum(rounded.astype(f32))
-        dctx_o[...] = mul(rounded, out_columns(place[3], wo, wo_2), LAST).astype(bf16)
+        dctx_o[...] = mul(rounded, columns(wo, 3, halves=(0, 1)), LAST).astype(bf16)
 
 
 def backward_specs(half):
+    first = HALF_STEPS * half
     ins = [
         whole((ROWS, D)),
-        pl.BlockSpec((ROWS, 384), lambda b, *_: (0, 4 * half + b)),
+        pl.BlockSpec((ROWS, STEP), lambda b: (0, first + b)),
         whole((ROWS, D)),
-        pl.BlockSpec((16, 1, 144, LANES), lambda b, *_: (0, half, b, 0)),
-        pl.BlockSpec((2, 2, 576, LANES), lambda b, *_: (4 * half + b, 0, 1, 0)),
+        pl.BlockSpec((16, 1, STEP * 3 // 8, LANES), lambda b: (0, half, b, 0)),
+        pl.BlockSpec((STEP // 192, 2, 576, LANES), lambda b: (first + b, 0, 1, 0)),
     ]
     outs = [
-        pl.BlockSpec((ROWS, 384), lambda b, *_: (0, 4 * half + b)),
-        pl.BlockSpec((8, 384), lambda b, *_: (0, 4 * half + b)),
+        pl.BlockSpec((ROWS, STEP), lambda b: (0, first + b)),
+        pl.BlockSpec((8, STEP), lambda b: (0, first + b)),
     ]
     return ins, outs, [shape((ROWS, FF), bf16), shape((8, FF))]
 
@@ -454,7 +446,7 @@
     ins, outs, shapes = backward_specs(0)
     return run(
         backward_one_kernel,
-        (4,),
+        (HALF_STEPS,),
         ins,
         outs + [kept((ROWS, D))],
         shapes + [shape((ROWS, D))],
@@ -463,21 +455,20 @@
     )(dbr, slope, dsec, gathered, gathered)
 
 
-def backward_two(place, dbr, slope, acc, n1, inv, vec, dpre, bi, gathered, own, other):
+def backward_two(dbr, slope, acc, n1, inv, vec, dpre, bi, gathered):
     wide, flat = shape((ROWS, D), bf16), whole((ROWS, D))
     ins, outs, shapes = backward_specs(1)
     return run(
         backward_two_kernel,
-        (4,),
-        ins + [OUT, OUT, flat, whole((ROWS, 1)), whole((8, D)), ANYWHERE, ANYWHERE],
+        (HALF_STEPS,),
+        ins + [OUT, flat, whole((ROWS, 1)), whole((8, D)), ANYWHERE, ANYWHERE],
         outs + [kept((ROWS, D)), kept((ROWS, D)), kept((ROWS, D)), kept((8, D))],
         shapes + [shape((ROWS, D)), wide, wide, shape((8, D))],
         [pltpu.VMEM((ROWS, D), f32)],
         flops=6_000_000_000,
         size=10_000_000,
-        alias={11: 0, 12: 1},
-        scalars=1,
-    )(place, dbr, slope, acc, gathered, gathered, own, other, n1, inv, vec, dpre, bi)
+        alias={9: 0, 10: 1},
+    )(dbr, slope, acc, gathered, gathered, gathered, n1, inv, vec, dpre, bi)
 
 
 def attend_back_kernel(
@@ -687,6 +678,37 @@
     return jax.tree.unflatten(tree, lax.optimization_barrier(tuple(flat)))
 
 
+def assemble_kernel(place, own, other, qkv, out, inw, back, row):
+    mine, theirs = own[...], other[...].astype(f32)
+    row[...] = mine[216:217] + theirs[216:217]
+    for core in range(2):
+
+        @pl.when(place[3] == core)
+        def _():
+            for half, rows in ((core, mine), (1 - core, theirs)):
+                blocks = [(qkv, 6 * t + 3 * half + j) for t in range(3) for j in range(3)]
+                blocks += [(out, 3 * half + j) for j in range(3)]
+                blocks += [(inw, 12 * half + j) for j in range(12)]
+                for i, (ref, j) in enumerate(blocks):
+                    ref[:, LANES * j : LANES * (j + 1)] = rows[6 * i : 6 * (i + 1)]
+                for i in range(3):
+                    j = 3 * half + i
+                    part = rows[144 + 24 * i : 144 + 24 * (i + 1)]
+                    back[:, LANES * j : LANES * (j + 1)] = part
+
+
+def assemble(place, own, other):
+    outs = [(6, 3 * D), (6, D), (6, FF), (24, D), (1, LANES)]
+    return run(
+        assemble_kernel,
+        (1,),
+        [kept((224, LANES))] * 2,
+        [kept(o) for o in outs],
+        [shape(o) for o in outs],
+        scalars=1,
+    )(place, own, other)
+
+
 def finish(place, core, parts):
     parts = around(last_sum(place, parts), "z")
     total = sum(p.astype(f32) for p in parts)
@@ -697,23 +719,12 @@
         a = lax.dynamic_index_in_dim(wide, which, 1, keepdims=False).reshape(144, LANES)
         b = lax.dynamic_index_in_dim(tall, which, 1, keepdims=False).reshape(72, LANES)
         row = lax.dynamic_index_in_dim(total[528:530], which, 0)
-        return jnp.concatenate([a, b, row], axis=0)
+        return jnp.concatenate([a, b, row, jnp.zeros((7, LANES), f32)], axis=0)
 
     own = for_core(core)
-    other = lax.ppermute(for_core(1 - core).astype(bf16), "c", shifted(2, 1)).astype(f32)
-    rows = own[216] + other[216]
-    left, right = jnp.where(core == 0, own, other), jnp.where(core == 0, other, own)
-
-    def joined(first, count, height, groups=1):
-        parts = [
-            jnp.moveaxis(a[first : first + count * height].reshape(count, height, LANES), 0, 1)
-            for a in (left, right)
-        ]
-        parts = [p.reshape(height, groups, -1) for p in parts]
-        return jnp.concatenate(parts, axis=2).reshape(height, -1)
-
-    weights = joined(0, 9, 6, 3), joined(54, 3, 6), joined(72, 12, 6), joined(144, 3, 24)
-    return weights, {n: rows[AT[n] : AT[n] + CUTS[n]] for n in NAMES}
+    other = swap(for_core(1 - core).astype(bf16))
+    *weights, rows = assemble(place, own, other)
+    return weights, {n: rows[0, AT[n] : AT[n] + CUTS[n]] for n in NAMES}
 
 
 def segment_rows(lengths, assignment, device, rows):
@@ -763,28 +774,29 @@
     ]
     px, py, pz, core = (lax.axis_index(a) for a in ("x", "y", "z", "c"))
     place = jnp.stack([px, py, pz, core]).astype(jnp.int32)
-    own, other, gathered = gather_all(
-        place, qkv_weight, out_weight, in_weight, back_weight, small
-    )
     segment = segment_rows(lengths, assignment, ((px * 4 + py) * 4 + pz) * 2 + core, ROWS)
     seg_col, seg_row = segment.reshape(ROWS, 1), segment.reshape(1, ROWS)
-    turned = hidden_in.T
-    q, k, v, lse, ctx, n1, low, low_t, inv, vec, bi = attend(
+    ready = (hidden_in.T, seg_col, seg_row)
+    own, other, gathered, ready = gather_all(
+        place, qkv_weight, out_weight, in_weight, back_weight, small, ready
+    )
+    turned, seg_col, seg_row = ready
+    q, k, v, lse, ctx_rows, ctx, vec, bi = attend(
         place, hidden_in, seg_col, seg_row, own, other
     )
-    turned_2, ctx_2, low_2 = swap(turned), swap(ctx), swap(low_t)
-    act, slope, layer_out, dsec, dbr, two = forward(
-        low, n1, seg_col, out_cotangent, vec, bi, gathered
-    )
-    act, dbr, turned_2, ctx_2, low_2 = together(act, dbr, turned_2, ctx_2, low_2)
-    act_2, dbr_2 = swap(act), swap(dbr)
+    turned_2, ctx_2 = swap(turned), swap(ctx)
+    act, slope, layer_out, dsec, dbr, two, n1, low, low_t, inv = forward(
+        hidden_in, ctx_rows, seg_col, out_cotangent, vec, bi, gathered
+    )
+    act, dbr, turned_2, ctx_2 = together(act, dbr, turned_2, ctx_2)
+    act_2, dbr_2, low_2 = swap(act), swap(dbr), swap(low_t)
     dpre, dbi, acc = backward_one(dbr, slope, dsec, gathered)
-    act_2, dbr_2, acc = together(act_2, dbr_2, acc)
+    act_2, dbr_2, low_2, acc = together(act_2, dbr_2, low_2, acc)
     back = back_grad(place, act, act_2, dbr, dbr_2)
     back, acc = together(back, acc)
     back = scattered(back.reshape(-1, LANES), "x")
     dpre, dbi, dfirst, dattn, dctx, one = backward_two(
-        place, dbr, slope, acc, n1, inv, vec, dpre, dbi, gathered, own, other
+        dbr, slope, acc, n1, inv, vec, dpre, dbi, gathered
     )
     dpre_2, dattn_2 = swap(dpre), swap(dattn)
     middle = middle_grad(

time: 280 us -> 271 us (0.968)
  Pallas kernels: 129 us -> 124 us
  waiting for transfers between devices: 49.5 us -> 45.7 us
    ppermute x15, waiting for transfers between devices: 20.9 us -> 13.6 us  [spread_along(): lax.ppermute(value, axis, shifted(4, k))]
    unnamed x50 -> x11, local copies, waits for them, and re-layouts: 8.25 us -> 4.49 us
    reduce_scatter x3, waiting for transfers between devices: 11.2 us -> 14.9 us  [scattered(): return lax.psum_scatter(value, axis, tiled=True)]
    pallas_call x1, Pallas kernels: 20.6 us -> 17.6 us  [attend(): run(attend_kernel, (6,), [whole((ROWS, D)), whole((ROWS, 1)), whole((1, R...]
    ppermute x1 -> x0, starting transfers between devices: 2.91 us -> none  [finish(): lax.ppermute(for_core(1 - core).astype(bf16), 'c', shifted(2, 1))]
    squeeze x0 -> x2, local copies, waits for them, and re-layouts: none -> 2.81 us  [finish(): return (weights, {n: rows[0, AT[n]:AT[n] + CUTS[n]] for n in NAMES})]
    ppermute x11 -> x12, starting transfers between devices: 11.1 us -> 12.9 us  [swap(): return lax.ppermute(value, 'c', shifted(2, 1))]
    pallas_call x4 -> x5, Pallas kernels: 41.5 us -> 40.4 us  [the longest x1 17.6 us: forward(): run(forward_kernel, (FF // STEP,), [flat, flat, whole((ROWS, 1)), flat, w...]
  transfers between devices with their start and end apart: 34 -> 34, of which waited for: 16 -> 20; matrix products, arithmetic and copies ran while one was open for 1% -> 3% of each run, Pallas kernels for 40% -> 38%
where the time goes in v1:
time: 271 us; the launch traced here: 270 us
  Pallas kernels  124 us (46%)
  waiting for transfers between devices  45.7 us (17%)
  starting transfers between devices  38.3 us (14%)
  blocking collectives  29.1 us (11%)
  between operations  14 us (5%)
  other arithmetic  9.52 us (4%)
  local copies, waits for them, and re-layouts  9.16 us (3%)
    all_to_all x1, blocking collectives, body(): lax.all_to_all(late, ('x', 'y'), 0, 0, tiled=True)  29.1 us
    pallas_call x2, Pallas kernels, attend_back(): run(functools.partial(attend_back_kernel, half), (3,), [pair, pair, pair,...  25.6 us
    ppermute x15, starting transfers between devices, spread_along(): lax.ppermute(value, axis, shifted(4, k))  20.9 us
    pallas_call x1, Pallas kernels, forward(): run(forward_kernel, (FF // STEP,), [flat, flat, whole((ROWS, 1)), flat, w...  17.6 us
    pallas_call x1, Pallas kernels, attend(): run(attend_kernel, (6,), [whole((ROWS, D)), whole((ROWS, 1)), whole((1, R...  17.6 us
    reduce_scatter x3, waiting for transfers between devices, scattered(): return lax.psum_scatter(value, axis, tiled=True)  14.9 us
    ppermute x15, waiting for transfers between devices, spread_along(): lax.ppermute(value, axis, shifted(4, k))  13.6 us
    ppermute x12, starting transfers between devices, swap(): return lax.ppermute(value, 'c', shifted(2, 1))  12.9 us
  transfers between devices with their start and end apart: 34, of which 20 were waited for; matrix products, arithmetic and copies ran while one was open for 3% of the time, Pallas kernels for 38%

profile of v1, /device:TPU:1, one launch (start us, length us, event | category | flops | bytes accessed | tf_op | source)
XLA Modules:
  0.0 269.8 jit_solution(10095750309952605640)
XLA Ops:
  24.7 2.6 shard_map.281
  36.6 2.9 %collective-permute-done.9.refs_7_ = bf16[224,128]{1,0:T(8,128)(2,1)} collective-permute-done((bf16[224,128]{1,0:T(8,128)(2,1)}, bf16[224,128]{1,0:T(8,128)(2,1)}, u32[]{:S(2)}, u32[]{:S(2)}) %collective-permute-start.9) | collective-permute-done | bytes 57376 | tf_op jit(solution)/shard_map/ppermute | solution.py:167
  46.6 2.7 collective-permute-start.11
  60.4 3.6 %shard_map.283.own = bf16[16,448,128]{2,1,0:T(8,128)(2,1)} custom-call(s32[4]{0:T(128)} %pad_add_fusion.place, bf16[4,224,128]{2,1,0:T(8,128)(2,1)} %get-tuple-element.101.refs_0_, bf16[4,224,128]{2,1,0:T(8,128)(2,1)} %collective-permute-done.10.refs_1_, bf16[4,224,128]{2,1,0:T(8,128)(2,1)} %collective-permute-done.11.refs_2_, ...), custom_call_target="tpu_custom_call" | custom-call | tf_op jit(solution)/shard_map/pallas_call | solution.py:156
  63.9 5.5 %collective-permute-start.16 = (bf16[16,448,128]{2,1,0:T(8,128)(2,1)}, bf16[16,448,128]{2,1,0:T(8,128)(2,1)}, u32[]{:S(2)}, u32[]{:S(2)}) collective-permute-start(bf16[16,448,128]{2,1,0:T(8,128)(2,1)} %shard_map.283.own), channel_id=1, source_target_pairs={{0,1},{1,0},{2,3},{3,2},{4,5},{5,4},{6,7},{7,6},{8,9},{9,8},{10,11... | collective-permute-start | bytes 5505032 | tf_op jit(solution)/shard_map/ppermute | solution.py:673
  71.0 2.5 collective-permute-done.16.other
  73.6 17.6 %shard_map.284 = (bf16[512,768]{1,0:T(8,128)(2,1)}, bf16[512,768]{1,0:T(8,128)(2,1)}, bf16[512,768]{1,0:T(8,128)(2,1)}, f32[6,8,512]{2,1,0:T(8,128)}, bf16[512,7...) custom-call(s32[4]{0:T(128)} %pad_add_fusion.place, bf16[512,768]{1,0:T(8,128)(2,1)} %x.21, ...), custom_call_target="tpu_custom_call" | custom-call | flops 6000000000 | bytes 12000000 | tf_op jit(solution)/shard_map/pallas_call | solution.py:314
  91.7 17.6 %shard_map.285 = (bf16[3072,512]{1,0:T(8,128)(2,1)}, bf16[512,3072]{1,0:T(8,128)(2,1)}, bf16[512,768]{1,0:T(8,128)(2,1)}, f32[512,768]{1,0:T(8,128)}, bf16[512,7...) custom-call(bf16[512,768]{1,0:T(8,128)(2,1)} %x.21, ...), custom_call_target="tpu_custom_call" | custom-call | flops 10000000000 | bytes 20000000 | tf_op jit(solution)/shard_map/pallas_call | solution.py:378
  110.2 7.4 %shard_map.286 = (bf16[512,3072]{1,0:T(8,128)(2,1)}, f32[8,3072]{1,0:T(8,128)}, f32[512,768]{1,0:T(8,128)}) custom-call(bf16[512,768]{1,0:T(8,128)(2,1)} %get-tuple-element.123.dbr, bf16[512,3072]{1,0:T(8,128)(2,1)} %get-tuple-element.124.slope, f32[512,768]{1,0:T(8,128)} %get-tuple-element.125.dsec, bf16[16,2,1296,128]{3,2,1,0:T(8,128)(2,1)} %bitcast.46, ...), custom_call_target="tpu_custom_call" | custom-call | flops 5000000000 | bytes 10000000 | tf_op jit(solution)/shard_map/pallas_call | solution.py:447
  117.7 9.6 %shard_map.287 = bf16[16,576,128]{2,1,0:T(8,128)(2,1)} custom-call(s32[4]{0:T(128)} %pad_add_fusion.place, bf16[3072,512]{1,0:T(8,128)(2,1)} %get-tuple-element.122.act, bf16[3072,512]{1,0:T(8,128)(2,1)} %collective-permute-done.19.act_2, bf16[512,768]{1,0:T(8,128)(2,1)} %get-tuple-element.123.dbr, bf16[512,768]{1,0:T(8,128)(2,1)} %collective-permute-done.20.dbr_2), custom_call_target="tpu_custom_call" | custom-call | flops 2400000000 | bytes 10000000 | tf_op jit(solution)/shard_map/pallas_call | solution.py:553
  127.4 10.4 %shard_map.288 = (bf16[512,3072]{1,0:T(8,128)(2,1)}, f32[8,3072]{1,0:T(8,128)}, f32[512,768]{1,0:T(8,128)}, bf16[512,768]{1,0:T(8,128)(2,1)}, bf16[512,768]{1,0:T(8,128)(2,1)}, /*index=5*/f32[8,768]{1,0:T(8,128)}) custom-call(bf16[512,768]{1,0:T(8,128)(2,1)} %get-tuple-element.123.dbr, ...), custom_call_target="tpu_custom_call", output_to_operand_aliasing={{0}: (9, {}), {1}: (10, {})} | custom-call | flops 6000000000 | bytes 10000000 | tf_op jit(solution)/shard_map/pallas_call | solution.py:461
  138.4 6.6 %collective-permute-done.23.dattn_2 = bf16[512,768]{1,0:T(8,128)(2,1)} collective-permute-done((bf16[512,768]{1,0:T(8,128)(2,1)}, bf16[512,768]{1,0:T(8,128)(2,1)}, u32[]{:S(2)}, u32[]{:S(2)}) %collective-permute-start.23) | collective-permute-done | bytes 786464 | tf_op jit(solution)/shard_map/ppermute | solution.py:673
  145.0 11.1 %shard_map.289 = bf16[16,736,128]{2,1,0:T(8,128)(2,1)} custom-call(s32[4]{0:T(128)} %pad_add_fusion.place, bf16[768,512]{1,0:T(8,128)(2,1)} %get-tuple-element.117.low, bf16[768,512]{1,0:T(8,128)(2,1)} %collective-permute-done.21.low_2, bf16[512,3072]{1,0:T(8,128)(2,1)} %get-tuple-element.136.dpre, bf16[512,3072]{1,0:T(8,128)(2,1)} %collective-permute-done.22.dpre_2, ...), custom_call_target="tpu_custom_call" | custom-call | flops 3200000000 | bytes 12000000 | tf_op jit(solution)/shard_map/pallas_call | solution.py:587
  156.2 13.1 %shard_map.290 = (bf16[3,512,384]{2,1,0:T(8,128)(2,1)}, f32[8,384]{1,0:T(8,128)}, f32[512,768]{1,0:T(8,128)}) custom-call(s32[4]{0:T(128)} %pad_add_fusion.place, bf16[512,768]{1,0:T(8,128)(2,1)} %get-tuple-element.114.q, bf16[512,768]{1,0:T(8,128)(2,1)} %get-tuple-element.115.k, bf16[512,768]{1,0:T(8,128)(2,1)} %get-tuple-element.116.v, ...), custom_call_target="tpu_custom_call" | custom-call | flops 6000000000 | bytes 8000000 | tf_op jit(solution)/shard_map/pallas_call | solution.py:521
  169.4 12.6 %shard_map.291 = (bf16[3,512,384]{2,1,0:T(8,128)(2,1)}, f32[8,384]{1,0:T(8,128)}, bf16[512,768]{1,0:T(8,128)(2,1)}) custom-call(s32[4]{0:T(128)} %pad_add_fusion.place, bf16[512,768]{1,0:T(8,128)(2,1)} %get-tuple-element.114.q, bf16[512,768]{1,0:T(8,128)(2,1)} %get-tuple-element.115.k, bf16[512,768]{1,0:T(8,128)(2,1)} %get-tuple-element.116.v, ...), custom_call_target="tpu_custom_call" | custom-call | flops 6000000000 | bytes 8000000 | tf_op jit(solution)/shard_map/pallas_call | solution.py:521
  182.7 2.8 %collective-permute-done.25.right_2 = bf16[3,512,384]{2,1,0:T(8,128)(2,1)} collective-permute-done((bf16[3,512,384]{2,1,0:T(8,128)(2,1)}, bf16[3,512,384]{2,1,0:T(8,128)(2,1)}, u32[]{:S(2)}, u32[]{:S(2)}) %collective-permute-start.25) | collective-permute-done | bytes 1179680 | tf_op jit(solution)/shard_map/ppermute | solution.py:673
  185.5 7.7 %shard_map.292 = bf16[16,448,128]{2,1,0:T(8,128)(2,1)} custom-call(s32[4]{0:T(128)} %pad_add_fusion.place, bf16[768,512]{1,0:T(8,128)(2,1)} %bitcast.55, bf16[768,512]{1,0:T(8,128)(2,1)} %collective-permute-done.17.x_2, bf16[3,512,384]{2,1,0:T(8,128)(2,1)} %get-tuple-element.151.left, bf16[3,512,384]{2,1,0:T(8,128)(2,1)} %collective-permute-done.24.left_2, ...), custom_call_target="tpu_custom_call" | custom-call | flops 1800000000 | bytes 7000000 | tf_op jit(solution)/shard_map/pallas_call | solution.py:614
  193.2 4.6 %reduce-scatter.6.cloned.1.call-done = bf16[2944,128]{1,0:T(8,128)(2,1)} async-done(((bf16[11776,128]{1,0:T(8,128)(2,1)}), bf16[2944,128]{1,0:T(8,128)(2,1)}) %reduce-scatter.6.cloned.1.call-update) | async-done | bytes 753680 | tf_op jit(solution)/shard_map/reduce_scatter | solution.py:669
  197.8 2.6 pad_maximum_fusion
  200.5 29.1 %all_to_all.5.refs_1_ = bf16[16,448,128]{2,1,0:T(8,128)(2,1)} all-to-all(bf16[16,448,128]{2,1,0:T(8,128)(2,1)S(1)} %copy-done), channel_id=1, replica_groups=mesh['x'=4,'y'=4,'z'=4,'c'=2] {'x','y'}, dimensions={0} | all-to-all | bytes 3670016 | tf_op jit(solution)/shard_map/all_to_all | solution.py:820
  229.5 10.4 %reduce-scatter.8.cloned.1.call-done.refs_0_ = bf16[1312,128]{1,0:T(8,128)(2,1)} async-done(((bf16[5248,128]{1,0:T(8,128)(2,1)}), bf16[1312,128]{1,0:T(8,128)(2,1)}) %reduce-scatter.8.cloned.1.call-update) | async-done | bytes 335888 | tf_op jit(solution)/shard_map/reduce_scatter | solution.py:669
  239.9 3.7 %shard_map.293 = (bf16[544,128]{1,0:T(8,128)(2,1)}, bf16[544,128]{1,0:T(8,128)(2,1)}, bf16[544,128]{1,0:T(8,128)(2,1)}, bf16[544,128]{1,0:T(8,128)(2,1)}) custom-call(s32[4]{0:T(128)} %pad_add_fusion.place, bf16[1312,128]{1,0:T(8,128)(2,1)} %reduce-scatter.8.cloned.1.call-done.refs_0_, bf16[16,448,128]{2,1,0:T(8,128)(2,1)} %all_to_all.5.refs_1_), custom_call_target="tpu_custom_call" | custom-call | bytes 4000000 | tf_op jit(solution)/shard_map/pallas_call | solution.py:653
  249.0 3.7 %collective-permute-done.28 = bf16[544,128]{1,0:T(8,128)(2,1)S(1)} collective-permute-done((bf16[544,128]{1,0:T(8,128)(2,1)}, bf16[544,128]{1,0:T(8,128)(2,1)S(1)}, u32[]{:S(2)}, u32[]{:S(2)}) %collective-permute-start.28) | collective-permute-done | bytes 139296 | tf_op jit(solution)/shard_map/ppermute | solution.py:665
  254.0 3.1 %collective-permute-start.29 = (bf16[224,128]{1,0:T(8,128)(2,1)S(1)}, bf16[224,128]{1,0:T(8,128)(2,1)}, u32[]{:S(2)}, u32[]{:S(2)}) collective-permute-start(bf16[224,128]{1,0:T(8,128)(2,1)S(1)} %maximum_maximum_fusion.1), channel_id=1, source_target_pairs={{0,1},{1,0},{2,3},{3,2},{4,5},{5,4},{6,7},{7,6},{8,9},{9,8},{10,11... | collective-permute-start | bytes 172040 | tf_op jit(solution)/shard_map/ppermute | solution.py:673
  (107 shorter events, 62.3 us)
Async XLA Ops:
  7.2 84.6 %all-gather.3.cloned.1.call-start = ((), (), s32[]{:S(2)}) async-start(), calls=%async_computation.7 | async-start | bytes 10948608 | tf_op jit(solution)/shard_map/all_gather | solution.py:175
  13.9 7.1 %collective-permute-start.1 = (bf16[448,128]{1,0:T(8,128)(2,1)S(1)}, bf16[448,128]{1,0:T(8,128)(2,1)S(1)}, u32[]{:S(2)}, u32[]{:S(2)}) collective-permute-start(bf16[448,128]{1,0:T(8,128)(2,1)S(1)} %constant_dynamic-update-slice_fusion.refs_0_), channel_id=1, source_target_pairs={{0,2},{2,4},{4,6},{6,0},{1,3},{3,5},{5,7},{7,1},{8,10},{10,12},{12... | collective-permute-start | bytes 344072 | tf_op jit(solution)/shard_map/ppermute | solution.py:167
  17.9 6.8 %collective-permute-start.3 = (bf16[448,128]{1,0:T(8,128)(2,1)S(1)}, bf16[448,128]{1,0:T(8,128)(2,1)}, u32[]{:S(2)}, u32[]{:S(2)}) collective-permute-start(bf16[448,128]{1,0:T(8,128)(2,1)S(1)} %constant_dynamic-update-slice_fusion.refs_0_), channel_id=1, source_target_pairs={{0,4},{2,6},{4,0},{6,2},{1,5},{3,7},{5,1},{7,3},{8,12},{10,14},{12... | collective-permute-start | bytes 344072 | tf_op jit(solution)/shard_map/ppermute | solution.py:167
  27.3 165.9 %reduce-scatter.4.cloned.1.call-start = ((), (), s32[]{:S(2)}) async-start(), calls=%async_computation.4 | async-start | bytes 2949120 | tf_op jit(solution)/shard_map/reduce_scatter | solution.py:669
  27.4 7.0 %collective-permute-start.4 = (bf16[224,128]{1,0:T(8,128)(2,1)}, bf16[224,128]{1,0:T(8,128)(2,1)}, u32[]{:S(2)}, u32[]{:S(2)}) collective-permute-start(bf16[224,128]{1,0:T(8,128)(2,1)} %get-tuple-element.95.refs_0_), channel_id=1, source_target_pairs={{0,32},{32,64},{64,96},{96,0},{1,33},{33,65},{65,97},{97,1},{2,34}... | collective-permute-start | bytes 172040 | tf_op jit(solution)/shard_map/ppermute | solution.py:167
  28.7 7.4 %collective-permute-start.5 = (bf16[224,128]{1,0:T(8,128)(2,1)}, bf16[224,128]{1,0:T(8,128)(2,1)}, u32[]{:S(2)}, u32[]{:S(2)}) collective-permute-start(bf16[224,128]{1,0:T(8,128)(2,1)} %get-tuple-element.95.refs_0_), channel_id=1, source_target_pairs={{0,96},{32,0},{64,32},{96,64},{1,97},{33,1},{65,33},{97,65},{2,98}... | collective-permute-start | bytes 172040 | tf_op jit(solution)/shard_map/ppermute | solution.py:167
  41.9 10.2 %collective-permute-start.10 = (bf16[4,224,128]{2,1,0:T(8,128)(2,1)}, bf16[4,224,128]{2,1,0:T(8,128)(2,1)}, u32[]{:S(2)}, u32[]{:S(2)}) collective-permute-start(bf16[4,224,128]{2,1,0:T(8,128)(2,1)} %get-tuple-element.101.refs_0_), channel_id=1, source_target_pairs={{0,8},{8,16},{16,24},{24,0},{1,9},{9,17},{17,25},{25,1},{2,10},{10... | collective-permute-start | bytes 688136 | tf_op jit(solution)/shard_map/ppermute | solution.py:167
  46.6 9.7 %collective-permute-start.11 = (bf16[4,224,128]{2,1,0:T(8,128)(2,1)}, bf16[4,224,128]{2,1,0:T(8,128)(2,1)}, u32[]{:S(2)}, u32[]{:S(2)}) collective-permute-start(bf16[4,224,128]{2,1,0:T(8,128)(2,1)} %get-tuple-element.101.refs_0_), channel_id=1, source_target_pairs={{0,24},{8,0},{16,8},{24,16},{1,25},{9,1},{17,9},{25,17},{2,26},{10... | collective-permute-start | bytes 688136 | tf_op jit(solution)/shard_map/ppermute | solution.py:167
  49.3 7.5 %collective-permute-start.12 = (bf16[4,224,128]{2,1,0:T(8,128)(2,1)}, bf16[4,224,128]{2,1,0:T(8,128)(2,1)}, u32[]{:S(2)}, u32[]{:S(2)}) collective-permute-start(bf16[4,224,128]{2,1,0:T(8,128)(2,1)} %get-tuple-element.101.refs_0_), channel_id=1, source_target_pairs={{0,16},{8,24},{16,0},{24,8},{1,17},{9,25},{17,1},{25,9},{2,18},{10... | collective-permute-start | bytes 688136 | tf_op jit(solution)/shard_map/ppermute | solution.py:167
  49.5 7.3 %collective-permute-start.13 = (bf16[4,224,128]{2,1,0:T(8,128)(2,1)}, bf16[4,224,128]{2,1,0:T(8,128)(2,1)}, u32[]{:S(2)}, u32[]{:S(2)}) collective-permute-start(bf16[4,224,128]{2,1,0:T(8,128)(2,1)} %get-tuple-element.105.refs_4_), channel_id=1, source_target_pairs={{0,32},{32,64},{64,96},{96,0},{1,33},{33,65},{65,97},{97,1},{2,34}... | collective-permute-start | bytes 688136 | tf_op jit(solution)/shard_map/ppermute | solution.py:167
  49.8 8.1 %collective-permute-start.14 = (bf16[4,224,128]{2,1,0:T(8,128)(2,1)}, bf16[4,224,128]{2,1,0:T(8,128)(2,1)}, u32[]{:S(2)}, u32[]{:S(2)}) collective-permute-start(bf16[4,224,128]{2,1,0:T(8,128)(2,1)} %get-tuple-element.105.refs_4_), channel_id=1, source_target_pairs={{0,96},{32,0},{64,32},{96,64},{1,97},{33,1},{65,33},{97,65},{2,98}... | collective-permute-start | bytes 688136 | tf_op jit(solution)/shard_map/ppermute | solution.py:167
  52.2 8.2 %collective-permute-start.15 = (bf16[4,224,128]{2,1,0:T(8,128)(2,1)}, bf16[4,224,128]{2,1,0:T(8,128)(2,1)}, u32[]{:S(2)}, u32[]{:S(2)}) collective-permute-start(bf16[4,224,128]{2,1,0:T(8,128)(2,1)} %get-tuple-element.105.refs_4_), channel_id=1, source_target_pairs={{0,64},{32,96},{64,0},{96,32},{1,65},{33,97},{65,1},{97,33},{2,66}... | collective-permute-start | bytes 688136 | tf_op jit(solution)/shard_map/ppermute | solution.py:167
  63.9 9.6 %collective-permute-start.16 = (bf16[16,448,128]{2,1,0:T(8,128)(2,1)}, bf16[16,448,128]{2,1,0:T(8,128)(2,1)}, u32[]{:S(2)}, u32[]{:S(2)}) collective-permute-start(bf16[16,448,128]{2,1,0:T(8,128)(2,1)} %shard_map.283.own), channel_id=1, source_target_pairs={{0,1},{1,0},{2,3},{3,2},{4,5},{5,4},{6,7},{7,6},{8,9},{9,8},{10,11... | collective-permute-start | bytes 5505032 | tf_op jit(solution)/shard_map/ppermute | solution.py:673
  71.0 38.4 %collective-permute-start.17 = (bf16[768,512]{1,0:T(8,128)(2,1)}, bf16[768,512]{1,0:T(8,128)(2,1)}, u32[]{:S(2)}, u32[]{:S(2)}) collective-permute-start(bf16[768,512]{1,0:T(8,128)(2,1)} %bitcast.54), channel_id=1, source_target_pairs={{0,1},{1,0},{2,3},{3,2},{4,5},{5,4},{6,7},{7,6},{8,9},{9,8},{10,11... | collective-permute-start | bytes 2359304 | tf_op jit(solution)/shard_map/ppermute | solution.py:673
  91.2 18.2 %collective-permute-start.18 = (bf16[768,512]{1,0:T(8,128)(2,1)}, bf16[768,512]{1,0:T(8,128)(2,1)}, u32[]{:S(2)}, u32[]{:S(2)}) collective-permute-start(bf16[768,512]{1,0:T(8,128)(2,1)} %get-tuple-element.121.ctx), channel_id=1, source_target_pairs={{0,1},{1,0},{2,3},{3,2},{4,5},{5,4},{6,7},{7,6},{8,9},{9,8},{10,11... | collective-permute-start | bytes 2359304 | tf_op jit(solution)/shard_map/ppermute | solution.py:673
  109.4 8.3 %collective-permute-start.19 = (bf16[3072,512]{1,0:T(8,128)(2,1)}, bf16[3072,512]{1,0:T(8,128)(2,1)}, u32[]{:S(2)}, u32[]{:S(2)}) collective-permute-start(bf16[3072,512]{1,0:T(8,128)(2,1)} %get-tuple-element.122.act), channel_id=1, source_target_pairs={{0,1},{1,0},{2,3},{3,2},{4,5},{5,4},{6,7},{7,6},{8,9},{9,8},{10,11... | collective-permute-start | bytes 9437192 | tf_op jit(solution)/shard_map/ppermute | solution.py:673
  109.7 8.0 %collective-permute-start.20 = (bf16[512,768]{1,0:T(8,128)(2,1)}, bf16[512,768]{1,0:T(8,128)(2,1)}, u32[]{:S(2)}, u32[]{:S(2)}) collective-permute-start(bf16[512,768]{1,0:T(8,128)(2,1)} %get-tuple-element.123.dbr), channel_id=1, source_target_pairs={{0,1},{1,0},{2,3},{3,2},{4,5},{5,4},{6,7},{7,6},{8,9},{9,8},{10,11... | collective-permute-start | bytes 2359304 | tf_op jit(solution)/shard_map/ppermute | solution.py:673
  110.0 7.7 %collective-permute-start.21 = (bf16[768,512]{1,0:T(8,128)(2,1)}, bf16[768,512]{1,0:T(8,128)(2,1)}, u32[]{:S(2)}, u32[]{:S(2)}) collective-permute-start(bf16[768,512]{1,0:T(8,128)(2,1)} %get-tuple-element.117.low), channel_id=1, source_target_pairs={{0,1},{1,0},{2,3},{3,2},{4,5},{5,4},{6,7},{7,6},{8,9},{9,8},{10,11... | collective-permute-start | bytes 2359304 | tf_op jit(solution)/shard_map/ppermute | solution.py:673
  127.3 70.5 %reduce-scatter.6.cloned.1.call-start = ((), (), s32[]{:S(2)}) async-start(), calls=%async_computation.5 | async-start | bytes 3768320 | tf_op jit(solution)/shard_map/reduce_scatter | solution.py:669
  137.8 7.2 %collective-permute-start.22 = (bf16[512,3072]{1,0:T(8,128)(2,1)}, bf16[512,3072]{1,0:T(8,128)(2,1)}, u32[]{:S(2)}, u32[]{:S(2)}) collective-permute-start(bf16[512,3072]{1,0:T(8,128)(2,1)} %get-tuple-element.136.dpre), channel_id=1, source_target_pairs={{0,1},{1,0},{2,3},{3,2},{4,5},{5,4},{6,7},{7,6},{8,9},{9,8},{10,11... | collective-permute-start | bytes 9437192 | tf_op jit(solution)/shard_map/ppermute | solution.py:673
  138.1 6.9 %collective-permute-start.23 = (bf16[512,768]{1,0:T(8,128)(2,1)}, bf16[512,768]{1,0:T(8,128)(2,1)}, u32[]{:S(2)}, u32[]{:S(2)}) collective-permute-start(bf16[512,768]{1,0:T(8,128)(2,1)} %get-tuple-element.138.dattn), channel_id=1, source_target_pairs={{0,1},{1,0},{2,3},{3,2},{4,5},{5,4},{6,7},{7,6},{8,9},{9,8},{10,11... | collective-permute-start | bytes 2359304 | tf_op jit(solution)/shard_map/ppermute | solution.py:673
  156.1 83.8 %reduce-scatter.8.cloned.1.call-start = ((), (), s32[]{:S(2)}) async-start(), calls=%async_computation.6 | async-start | bytes 1679360 | tf_op jit(solution)/shard_map/reduce_scatter | solution.py:669
  169.2 12.7 %collective-permute-start.24 = (bf16[3,512,384]{2,1,0:T(8,128)(2,1)}, bf16[3,512,384]{2,1,0:T(8,128)(2,1)}, u32[]{:S(2)}, u32[]{:S(2)}) collective-permute-start(bf16[3,512,384]{2,1,0:T(8,128)(2,1)} %get-tuple-element.151.left), channel_id=1, source_target_pairs={{0,1},{1,0},{2,3},{3,2},{4,5},{5,4},{6,7},{7,6},{8,9},{9,8},{10,11... | collective-permute-start | bytes 3538952 | tf_op jit(solution)/shard_map/ppermute | solution.py:673
  246.3 6.4 %collective-permute-start.28 = (bf16[544,128]{1,0:T(8,128)(2,1)}, bf16[544,128]{1,0:T(8,128)(2,1)S(1)}, u32[]{:S(2)}, u32[]{:S(2)}) collective-permute-start(bf16[544,128]{1,0:T(8,128)(2,1)} %get-tuple-element.165), channel_id=1, source_target_pairs={{0,4},{2,6},{4,0},{6,2},{1,5},{3,7},{5,1},{7,3},{8,12},{10,14},{12... | collective-permute-start | bytes 417800 | tf_op jit(solution)/shard_map/ppermute | solution.py:665
  (14 other events, 52.2 us)
Sparse Core Ops, SparseCore 0:
  27.5 63.3 all-gather.2
  127.4 30.9 reduce-scatter.3
  160.9 36.8 reduce-scatter.5
  200.6 39.2 reduce-scatter.7
